TPU v7x, 256 devices: a whole 4x4x8 slice. The times are simulated.
256 devices in a mesh: seq: 8 (over x, core), tensor: 8 (over z), dp: 4 (over y).
Axes of the slice: x: 4, y: 4, z: 8, core: 2. Of those that a mesh axis runs over, the one named last changes fastest.
Arguments:
- span_act: bfloat16 [8192, 8192], P(('seq', 'dp'), 'tensor'), may hold values from -6 to 6
- q_weight: bfloat16 [8192, 4096], P(('seq', 'dp'), 'tensor'), may hold values from -0.0625 to 0.0625
- out_grad: bfloat16 [8192, 4096], P(('seq', 'dp'), 'tensor'), may hold values from -6 to 6
- neighbour_kv: bfloat16 [256, 2, 256, 4096], P(('seq', 'dp'), None, None, 'tensor'), may hold values from -210 to 210
- neighbour_ids: int32 [256, 256], P(('seq', 'dp')), may hold values from 0 to 255999, as said below
- owner: int32 [128], replicated, may hold values from 0 to 7, as said below
Outputs:
- act_grad: bfloat16 [8192, 8192], P(('seq', 'dp'), 'tensor')
- weight_grad: float32 [8192, 4096], P(('seq', 'dp'), 'tensor')
- kv_grad: bfloat16 [256, 2, 256, 4096], P(('seq', 'dp'), None, None, 'tensor')
Inputs may be any that keep to these rules, and one draw needn't show every extreme that they name: owner[c] is the owner's index along seq within span c's own dp group. Of the 4 spans of one home block at most 1 name the same owner, and in each dp group some owner is named by 1 spans of every home block. `neighbour_ids`: each of the 2 neighbours of a slot takes 128 consecutive positions; its ids are positive on a leading run of 32 to 128 positions and 0 (padding) after it. Slots that no span names are never read.
All inputs are finite; a program needn't handle non-finite values.
Results may differ from a plain program's by a relative error of at most 0.022.
The roundings to bfloat16 on the way count: a program that leaves them out, or rounds other values in their place, can miss the bound.
Values may be sent and summed in bfloat16 or wider, within the bound.
A program may use at most 128 MiB of HBM per device.

v0:
```python
import jax
import jax.numpy as jnp
from jax import lax
from jax.sharding import PartitionSpec as P

HD = 128
SPAN = 64
KEYS = 256


def attend_back(queries, grads, pair_kv, live):
    slots, rows, width = queries.shape
    heads = width // HD
    scale = HD ** (-0.5)
    query_heads = queries.reshape(slots, rows, heads, HD)
    grad_heads = grads.reshape(slots, rows, heads, HD)
    key_heads = pair_kv[:, 0].reshape(slots, -1, heads, HD)
    value_heads = pair_kv[:, 1].reshape(slots, -1, heads, HD)
    scores = (
        jnp.einsum("bqhd,bkhd->bhqk", query_heads, key_heads, preferred_element_type=jnp.float32)
        * scale
    )
    scores = jnp.where(live[:, None, None, :], scores, -1e30)
    top = jnp.max(scores, axis=-1, keepdims=True)
    expo = jnp.exp(scores - top)
    probs = expo / jnp.sum(expo, axis=-1, keepdims=True)
    value_grad = jnp.einsum(
        "bhqk,bqhd->bkhd",
        probs.astype(jnp.bfloat16),
        grad_heads,
        preferred_element_type=jnp.float32,
    )
    prob_grad = jnp.einsum(
        "bqhd,bkhd->bhqk", grad_heads, value_heads, preferred_element_type=jnp.float32
    )
    center = jnp.sum(probs * prob_grad, axis=-1, keepdims=True)
    score_grad = (probs * (prob_grad - center) * scale).astype(jnp.bfloat16)
    query_grad = jnp.einsum(
        "bhqk,bkhd->bqhd", score_grad, key_heads, preferred_element_type=jnp.float32
    )
    key_grad = jnp.einsum(
        "bhqk,bqhd->bkhd", score_grad, query_heads, preferred_element_type=jnp.float32
    )
    both = jnp.stack([key_grad.astype(jnp.bfloat16), value_grad.astype(jnp.bfloat16)], axis=1)
    return (
        query_grad.astype(jnp.bfloat16).reshape(slots, rows, width),
        both.reshape(slots, 2, -1, width),
    )


def on_device(span_act, q_weight, out_grad, neighbour_kv, neighbour_ids, owner):
    tok_rows = out_grad.shape[0]
    width = out_grad.shape[1]
    seq_count = lax.axis_size("seq")
    dp_count = lax.axis_size("dp")
    spans_dev = tok_rows // SPAN
    capacity = neighbour_kv.shape[0]
    pairs = capacity // seq_count
    block = lax.axis_index("seq") * dp_count + lax.axis_index("dp")
    whole = lax.all_gather(span_act, "tensor", axis=1, tiled=True)
    weights = lax.all_gather(q_weight, ("seq", "dp"), axis=0, tiled=True)
    queries = jnp.dot(whole, weights, preferred_element_type=jnp.float32).astype(jnp.bfloat16)
    mine = lax.dynamic_slice_in_dim(owner, block * spans_dev, spans_dev)
    position = jnp.arange(spans_dev)
    same = mine[:, None] == mine[None, :]
    before = position[None, :] < position[:, None]
    rank = jnp.sum(same & before, axis=1)
    target = mine * pairs + rank
    select = (jnp.arange(capacity)[:, None] == target[None, :]).astype(jnp.bfloat16)
    q_spans = queries.reshape(spans_dev, SPAN, width)
    g_spans = out_grad.reshape(spans_dev, SPAN, width)
    kv_recv, ids_recv = (
        lax.all_to_all(
            neighbour_kv.reshape(seq_count, pairs, 2, KEYS, width),
            "seq",
            split_axis=0,
            concat_axis=0,
            tiled=True,
        ),
        lax.all_to_all(
            neighbour_ids.reshape(seq_count, pairs, KEYS),
            "seq",
            split_axis=0,
            concat_axis=0,
            tiled=True,
        ),
    )
    flat_kv = kv_recv.reshape(capacity, 2 * KEYS * width)
    span_kv = jnp.einsum("sc,sf->cf", select, flat_kv, preferred_element_type=jnp.float32).astype(
        jnp.bfloat16
    )
    live_recv = (ids_recv.reshape(capacity, KEYS) != 0).astype(jnp.int32)
    span_live = jnp.sum(select.astype(jnp.int32)[:, :, None] * live_recv[:, None, :], axis=0) > 0
    query_grad, span_kv_grad = attend_back(
        q_spans, g_spans, span_kv.reshape(spans_dev, 2, KEYS, width), span_live
    )
    slot_kv_grad = jnp.einsum(
        "sc,cf->sf",
        select,
        span_kv_grad.reshape(spans_dev, 2 * KEYS * width),
        preferred_element_type=jnp.float32,
    ).astype(jnp.bfloat16)
    kv_grad = lax.all_to_all(
        slot_kv_grad.reshape(seq_count, pairs, 2, KEYS, width),
        "seq",
        split_axis=0,
        concat_axis=0,
        tiled=True,
    ).reshape(capacity, 2, KEYS, width)
    flat_grad = query_grad.reshape(tok_rows, width)
    partial_act = lax.dot_general(
        flat_grad, weights, (((1,), (1,)), ((), ())), preferred_element_type=jnp.float32
    )
    act_grad = lax.psum_scatter(
        partial_act.astype(jnp.bfloat16), "tensor", scatter_dimension=1, tiled=True
    )
    weight_grad = lax.psum_scatter(
        lax.dot_general(
            whole, flat_grad, (((0,), (0,)), ((), ())), preferred_element_type=jnp.float32
        ).astype(jnp.bfloat16),
        ("seq", "dp"),
        scatter_dimension=0,
        tiled=True,
    ).astype(jnp.float32)
    return (act_grad, weight_grad, kv_grad)


def solution(mesh):
    in_specs = (
        P(("seq", "dp"), "tensor"),
        P(("seq", "dp"), "tensor"),
        P(("seq", "dp"), "tensor"),
        P(("seq", "dp"), None, None, "tensor"),
        P(("seq", "dp"), None),
        P(),
    )
    out_specs = (
        P(("seq", "dp"), "tensor"),
        P(("seq", "dp"), "tensor"),
        P(("seq", "dp"), None, None, "tensor"),
    )
    return jax.shard_map(
        on_device, mesh=mesh, in_specs=in_specs, out_specs=out_specs, check_vma=False
    )
```

profile of v0, /device:TPU:2, one launch (start us, length us, event | category | flops | bytes accessed | tf_op | source)
XLA Modules:
  0.0 342.5 jit_solution(13357944711207713905)
XLA Ops:
  7.2 0.0 all-gather.3.cloned.1.call-start
  7.2 0.7 all-gather.3.cloned.1.call-update
  7.9 0.0 all-gather.5.cloned.1.call-start
  7.9 0.7 all-gather.5.cloned.1.call-update
  8.6 0.7 reshape.55
  9.4 8.5 %all_to_all.15 = s32[8,1,256]{2,1,0:T(1,128)S(1)} all-to-all(s32[8,1,256]{2,1,0:T(1,128)S(1)} %reshape.55), channel_id=1, replica_groups=mesh['seq'=8,'tensor'=8,'dp'=4] {'seq'}, dimensions={0} | all-to-all | bytes 16384 | tf_op jit(solution)/shard_map/all_to_all | solution.py:80
  17.8 6.0 %all-to-all-start = ((bf16[8,1,2,256,512]{4,3,2,1,0:T(8,128)(2,1)}), bf16[8,1,2,256,512]{4,3,2,1,0:T(8,128)(2,1)}, u32[]{:S(2)}, u32[]{:S(2)}) async-start(bf16[8,1,2,256,512]{4,3,2,1,0:T(8,128)(2,1)} %bitcast.51), calls=%async_computation | async-start | bytes 8388608 | tf_op jit(solution)/shard_map/all_to_all | solution.py:73
  23.8 0.0 reduce-scatter.5.cloned.1.call-start
  23.8 0.0 copy-done.1
  23.9 0.1 reshape_reshape.13
  23.9 0.1 dynamic_slice.3
  24.0 0.2 convert_reduce_fusion
  24.2 0.1 dynamic-slice_add_fusion
  24.3 0.1 fusion.31
  24.4 0.1 multiply_reduce_fusion.1
  24.5 47.7 %all-to-all-done = bf16[8,1,2,256,512]{4,3,2,1,0:T(8,128)(2,1)} async-done(((bf16[8,1,2,256,512]{4,3,2,1,0:T(8,128)(2,1)}), bf16[8,1,2,256,512]{4,3,2,1,0:T(8,128)(2,1)}, u32[]{:S(2)}, u32[]{:S(2)}) %all-to-all-start) | async-done | bytes 4194336 | tf_op jit(solution)/shard_map/all_to_all | solution.py:73
  72.2 4.5 %copy.65 = bf16[1,8,512,512]{3,1,2,0:T(8,128)(2,1)S(1)} copy(bf16[1,8,512,512]{3,2,1,0:T(8,128)(2,1)} %bitcast.16) | data formatting | bytes 8388608
  76.7 1.3 convolution_convert_fusion.1
  78.0 0.4 copy.66
  78.4 0.2 fusion.38
  78.7 0.5 copy.63
  79.2 0.5 copy.64
  79.7 1.3 convolution_bitcast_fusion
  81.0 45.7 %all-gather.5.cloned.1.call-done = bf16[8192,512]{1,0:T(8,128)(2,1)} async-done(((bf16[256,512]{1,0:T(8,128)(2,1)}), bf16[8192,512]{1,0:T(8,128)(2,1)}) %all-gather.5.cloned.1.call-update) | async-done | bytes 8388624 | tf_op jit(solution)/shard_map/all_gather | solution.py:61
  126.7 7.0 %convolution_convert_fusion.7 = bf16[256,512]{1,0:T(8,128)(2,1)S(1)} fusion(bf16[256,8192]{1,0:T(8,128)(2,1)} %all-gather.3.cloned.1.call-done, bf16[8192,512]{1,0:T(8,128)(2,1)} %all-gather.5.cloned.1.call-done), kind=kOutput, calls=%fused_computation.22 | convolution fusion | flops 2147614720 | bytes 12845056 | tf_op jit(solution)/shard_map/dot_general | solution.py:62
  133.7 0.1 reshape_reshape.12
  133.7 0.3 fusion.10
  134.1 1.2 fusion.39
  135.3 7.6 %fusion.12 = bf16[4,64,4,128]{3,1,2,0:T(8,128)(2,1)S(1)} fusion(bf16[4,256,4,128]{1,3,2,0:T(8,128)(2,1)S(1)} %bitcast.53, f32[4,4,64,256]{3,2,1,0:T(8,128)} %convolution_bitcast_fusion, f32[4,4,64,256]{3,2,1,0:T(8,128)} %get-tuple-element.18, f32[4,4,64]{2,1,0:T(4,128)S(1)} %get-tuple-element.17), kind=kOutput, calls=%fused_computation.23 | convolution fusion | flops 69076224 | bytes 3411968 | tf_op jit(solution)/shard_map/bhqk,bkhd->bqhd/dot_general | solution.py:38
  142.9 0.2 copy.51
  143.2 7.8 %fusion.2 = bf16[8192,512]{0,1:T(8,128)(2,1)} fusion(bf16[256,8192]{1,0:T(8,128)(2,1)} %all-gather.3.cloned.1.call-done, bf16[32,8,4,128]{3,2,1,0:T(4,128)(2,1)S(1)} %bitcast.55), kind=kOutput, calls=%fused_computation.5 | convolution fusion | flops 2151677952 | bytes 12845056 | tf_op jit(solution)/shard_map/dot_general | solution.py:118
  151.0 0.0 reduce-scatter.5.cloned.1.call-update
  151.0 0.2 reduce-scatter.3.cloned.1.call-start
  151.2 7.8 %convolution_convert_fusion.3 = bf16[256,8192]{1,0:T(8,128)(2,1)} fusion(bf16[8192,512]{1,0:T(8,128)(2,1)} %all-gather.5.cloned.1.call-done, bf16[32,8,4,128]{3,2,1,0:T(4,128)(2,1)S(1)} %bitcast.56), kind=kOutput, calls=%fused_computation.6 | convolution fusion | flops 2149580800 | bytes 12845056 | tf_op jit(solution)/shard_map/dot_general | solution.py:111
  159.0 0.0 reduce-scatter.3.cloned.1.call-update
  159.0 9.0 %fusion.4 = bf16[4,1,256,4,128]{2,4,3,0,1:T(8,128)(2,1)} fusion(f32[4,4,64,256]{3,2,1,0:T(8,128)} %convolution_bitcast_fusion, bf16[4,64,4,128]{3,2,1,0:T(4,128)(2,1)S(1)} %reshape_reshape.12, f32[4,4,64,256]{3,2,1,0:T(8,128)} %get-tuple-element.18, f32[4,4,64]{2,1,0:T(4,128)S(1)} %get-tuple-element.17), kind=kOutput, calls=%fused_computation.11 | convolution fusion | flops 69469440 | bytes 3411968 | tf_op jit(solution)/shard_map/bhqk,bqhd->bkhd/dot_general | solution.py:41
  168.0 3.1 fusion.5
  171.1 0.0 copy-done
  171.1 1.5 pad_maximum_fusion
  172.6 2.5 copy.55
  175.1 2.5 reshape_reshape.15
  177.6 1.9 convolution_convert_fusion
  179.4 1.4 copy.56
  180.8 70.2 %all_to_all.16 = bf16[8,1,2,256,512]{4,3,2,1,0:T(8,128)(2,1)} all-to-all(bf16[8,1,2,256,512]{4,3,2,1,0:T(8,128)(2,1)S(1)} %copy.56), channel_id=1, replica_groups=mesh['seq'=8,'tensor'=8,'dp'=4] {'seq'}, dimensions={0} | all-to-all | bytes 8388608 | tf_op jit(solution)/shard_map/all_to_all | solution.py:103
  251.0 22.2 %reduce-scatter.5.cloned.1.call-done = bf16[256,512]{0,1:T(8,128)(2,1)} async-done(((bf16[8192,512]{0,1:T(8,128)(2,1)}), bf16[256,512]{0,1:T(8,128)(2,1)}) %reduce-scatter.5.cloned.1.call-update) | async-done | bytes 262160 | tf_op jit(solution)/shard_map/reduce_scatter | solution.py:117
  273.2 1.9 copy.57
  275.1 56.3 %reduce-scatter.3.cloned.1.call-done = bf16[256,1024]{1,0:T(8,128)(2,1)} async-done(((bf16[256,8192]{1,0:T(8,128)(2,1)}), bf16[256,1024]{1,0:T(8,128)(2,1)}) %reduce-scatter.3.cloned.1.call-update) | async-done | bytes 524304 | tf_op jit(solution)/shard_map/reduce_scatter | solution.py:114
  331.4 4.6 %copy.87 = bf16[8,2,256,512]{3,2,1,0:T(8,128)(2,1)} copy(bf16[8,2,256,512]{3,2,1,0:T(8,128)(2,1)} %bitcast.48) | data formatting | bytes 8388608
  (8 shorter events, 0.0 us)
Async XLA Ops:
  7.2 73.8 %all-gather.3.cloned.1.call-start = ((), (), s32[]{:S(2)}) async-start(), calls=%async_computation.5 | async-start | bytes 4718592 | tf_op jit(solution)/shard_map/all_gather | solution.py:60
  7.9 118.8 %all-gather.5.cloned.1.call-start = ((), (), s32[]{:S(2)}) async-start(), calls=%async_computation.6 | async-start | bytes 8650752 | tf_op jit(solution)/shard_map/all_gather | solution.py:61
  17.8 6.0 %copy-start.1 = (bf16[256,512]{1,0:T(8,128)(2,1)S(1)}, bf16[256,512]{1,0:T(8,128)(2,1)}, u32[]{:S(2)}) copy-start(bf16[256,512]{1,0:T(8,128)(2,1)} %param.8) | copy-start | bytes 786436
  17.8 6.1 %copy-start.2 = (s32[128]{0:T(128)S(1)}, s32[128]{0:T(128)}, u32[]{:S(2)}) copy-start(s32[128]{0:T(128)} %param.11) | copy-start | bytes 1540
  17.8 54.4 %all-to-all-start = ((bf16[8,1,2,256,512]{4,3,2,1,0:T(8,128)(2,1)}), bf16[8,1,2,256,512]{4,3,2,1,0:T(8,128)(2,1)}, u32[]{:S(2)}, u32[]{:S(2)}) async-start(bf16[8,1,2,256,512]{4,3,2,1,0:T(8,128)(2,1)} %bitcast.51), calls=%async_computation | async-start | bytes 8388608 | tf_op jit(solution)/shard_map/all_to_all | solution.py:73
  23.8 249.3 %reduce-scatter.5.cloned.1.call-start = ((), (), s32[]{:S(2)}) async-start(), calls=%async_computation.8 | async-start | bytes 8650752 | tf_op jit(solution)/shard_map/reduce_scatter | solution.py:117
  151.0 180.4 %reduce-scatter.3.cloned.1.call-start = ((), (), s32[]{:S(2)}) async-start(), calls=%async_computation.7 | async-start | bytes 4718592 | tf_op jit(solution)/shard_map/reduce_scatter | solution.py:114
  168.0 3.1 copy-start
Sparse Core Ops, SparseCore 0:
  9.8 57.7 all-gather.2
  70.2 56.4 all-gather.4
  151.1 122.0 reduce-scatter.4
  276.3 55.0 reduce-scatter.2
where the time goes:
time: 344 us; the launch traced here: 342 us
  waiting for transfers between devices  173 us (50%)
  blocking collectives  78.7 us (23%)
  matrix products  47 us (14%)
  local copies, waits for them, and re-layouts  20.2 us (6%)
  between operations  13.9 us (4%)
  starting transfers between devices  6.32 us (2%)
    all_to_all x1, blocking collectives, on_device(): lax.all_to_all(slot_kv_grad.reshape(seq_count, pairs, 2, KEYS, width), 's...  70.2 us
    reduce_scatter x1, waiting for transfers between devices, on_device(): lax.psum_scatter(partial_act.astype(jnp.bfloat16), 'tensor', scatter_dime...  56.3 us
    all_to_all x1, waiting for transfers between devices, on_device(): lax.all_to_all(neighbour_kv.reshape(seq_count, pairs, 2, KEYS, width), 's...  47.7 us
    all_gather x1, waiting for transfers between devices, on_device(): weights = lax.all_gather(q_weight, ('seq', 'dp'), axis=0, tiled=True)  45.7 us
    reduce_scatter x1, waiting for transfers between devices, on_device(): lax.psum_scatter(lax.dot_general(whole, flat_grad, (((0,), (0,)), ((), ()...  22.2 us
    unnamed x13, local copies, waits for them, and re-layouts  12.5 us
    dot_general x1, matrix products, attend_back(): jnp.einsum('bhqk,bqhd->bkhd', score_grad, query_heads, preferred_element_...  9.03 us
    all_to_all x1, blocking collectives, on_device(): lax.all_to_all(neighbour_ids.reshape(seq_count, pairs, KEYS), 'seq', spli...  8.47 us
  transfers between devices with their start and end apart: 5, of which 4 were waited for; matrix products, arithmetic and copies ran while one was open for 12% of the time, Pallas kernels for 0%

commit v1 on v0

--- a/solution.py
+++ b/solution.py
@@ -66,47 +66,34 @@
     before = position[None, :] < position[:, None]
     rank = jnp.sum(same & before, axis=1)
     target = mine * pairs + rank
-    select = (jnp.arange(capacity)[:, None] == target[None, :]).astype(jnp.bfloat16)
-    q_spans = queries.reshape(spans_dev, SPAN, width)
-    g_spans = out_grad.reshape(spans_dev, SPAN, width)
-    kv_recv, ids_recv = (
-        lax.all_to_all(
-            neighbour_kv.reshape(seq_count, pairs, 2, KEYS, width),
+    select = jnp.arange(capacity)[:, None] == target[None, :]
+
+    def to_owner(rows):
+        spans = rows.reshape(spans_dev, SPAN, width)
+        slots = jnp.zeros((capacity, SPAN, width), rows.dtype)
+        for c in range(spans_dev):
+            slots = jnp.where(select[:, c][:, None, None], spans[c][None], slots)
+        return lax.all_to_all(
+            slots.reshape(seq_count, pairs, SPAN, width),
             "seq",
             split_axis=0,
             concat_axis=0,
             tiled=True,
-        ),
-        lax.all_to_all(
-            neighbour_ids.reshape(seq_count, pairs, KEYS),
-            "seq",
-            split_axis=0,
-            concat_axis=0,
-            tiled=True,
-        ),
-    )
-    flat_kv = kv_recv.reshape(capacity, 2 * KEYS * width)
-    span_kv = jnp.einsum("sc,sf->cf", select, flat_kv, preferred_element_type=jnp.float32).astype(
-        jnp.bfloat16
-    )
-    live_recv = (ids_recv.reshape(capacity, KEYS) != 0).astype(jnp.int32)
-    span_live = jnp.sum(select.astype(jnp.int32)[:, :, None] * live_recv[:, None, :], axis=0) > 0
-    query_grad, span_kv_grad = attend_back(
-        q_spans, g_spans, span_kv.reshape(spans_dev, 2, KEYS, width), span_live
-    )
-    slot_kv_grad = jnp.einsum(
-        "sc,cf->sf",
-        select,
-        span_kv_grad.reshape(spans_dev, 2 * KEYS * width),
-        preferred_element_type=jnp.float32,
-    ).astype(jnp.bfloat16)
-    kv_grad = lax.all_to_all(
-        slot_kv_grad.reshape(seq_count, pairs, 2, KEYS, width),
+        ).reshape(capacity, SPAN, width)
+
+    g_slots = to_owner(out_grad)
+    q_slots = to_owner(queries)
+    slot_grad, kv_grad = attend_back(q_slots, g_slots, neighbour_kv, neighbour_ids != 0)
+    home_grad = lax.all_to_all(
+        slot_grad.reshape(seq_count, pairs, SPAN, width),
         "seq",
         split_axis=0,
         concat_axis=0,
         tiled=True,
-    ).reshape(capacity, 2, KEYS, width)
+    ).reshape(capacity, SPAN, width)
+    query_grad = jnp.zeros((spans_dev, SPAN, width), home_grad.dtype)
+    for s in range(capacity):
+        query_grad = jnp.where(select[s][:, None, None], home_grad[s][None], query_grad)
     flat_grad = query_grad.reshape(tok_rows, width)
     partial_act = lax.dot_general(
         flat_grad, weights, (((1,), (1,)), ((), ())), preferred_element_type=jnp.float32

time: 344 us -> 380 us (1.10)
  blocking collectives: 78.7 us -> 0 us
  waiting for transfers between devices: 173 us -> 245 us
  matrix products: 47 us -> 64.3 us
  local copies, waits for them, and re-layouts: 20.2 us -> 31.4 us
  starting transfers between devices: 6.32 us -> 15.4 us
  other arithmetic: 3.14 us -> 8.5 us
    all_to_all x2 -> x0, blocking collectives: 78.7 us -> none  [the longest x1 70.2 us: on_device(): lax.all_to_all(slot_kv_grad.reshape(seq_count, pairs, 2, KEYS, width), 's...]
    all_gather x1, waiting for transfers between devices: 0.01 us -> 56.1 us  [on_device(): whole = lax.all_gather(span_act, 'tensor', axis=1, tiled=True)]
    reduce_scatter x1, waiting for transfers between devices: 22.2 us -> 57.3 us  [on_device(): lax.psum_scatter(lax.dot_general(whole, flat_grad, (((0,), (0,)), ((), ()...]
    all_to_all x1 -> x3, waiting for transfers between devices: 47.7 us -> 14.8 us  [the longest x1 7.72 us: on_device(): lax.all_to_all(slot_grad.reshape(seq_count, pairs, SPAN, width), 'seq', s...]
    all_gather x1, waiting for transfers between devices: 45.7 us -> 59.1 us  [on_device(): weights = lax.all_gather(q_weight, ('seq', 'dp'), axis=0, tiled=True)]
    all_to_all x1 -> x3, starting transfers between devices: 6.02 us -> 15.1 us  [the longest x2 9.61 us: to_owner(): lax.all_to_all(slots.reshape(seq_count, pairs, SPAN, width), 'seq', split...]
    dot_general x1, matrix products: 7.65 us -> 16.1 us  [attend_back(): jnp.einsum('bhqk,bkhd->bqhd', score_grad, key_heads, preferred_element_ty...]
    dot_general x1, matrix products: 9.03 us -> 16.7 us  [attend_back(): jnp.einsum('bhqk,bqhd->bkhd', score_grad, query_heads, preferred_element_...]
  transfers between devices with their start and end apart: 5 -> 7, of which waited for: 4 -> 6; matrix products, arithmetic and copies ran while one was open for 12% -> 16% of each run, Pallas kernels for 0% -> 0%
where the time goes in v1:
time: 380 us; the launch traced here: 378 us
  waiting for transfers between devices  245 us (64%)
  matrix products  64.3 us (17%)
  local copies, waits for them, and re-layouts  31.4 us (8%)
  starting transfers between devices  15.4 us (4%)
  between operations  13.9 us (4%)
  other arithmetic  8.5 us (2%)
    all_gather x1, waiting for transfers between devices, on_device(): weights = lax.all_gather(q_weight, ('seq', 'dp'), axis=0, tiled=True)  59.1 us
    reduce_scatter x1, waiting for transfers between devices, on_device(): lax.psum_scatter(lax.dot_general(whole, flat_grad, (((0,), (0,)), ((), ()...  57.3 us
    reduce_scatter x1, waiting for transfers between devices, on_device(): lax.psum_scatter(partial_act.astype(jnp.bfloat16), 'tensor', scatter_dime...  56.3 us
    all_gather x1, waiting for transfers between devices, on_device(): whole = lax.all_gather(span_act, 'tensor', axis=1, tiled=True)  56.1 us
    dot_general x1, matrix products, attend_back(): jnp.einsum('bhqk,bqhd->bkhd', score_grad, query_heads, preferred_element_...  16.7 us
    dot_general x1, matrix products, attend_back(): jnp.einsum('bhqk,bkhd->bqhd', score_grad, key_heads, preferred_element_ty...  16.1 us
    all_to_all x2, starting transfers between devices, to_owner(): lax.all_to_all(slots.reshape(seq_count, pairs, SPAN, width), 'seq', split...  9.61 us
    unnamed x7, local copies, waits for them, and re-layouts  8.65 us
  transfers between devices with their start and end apart: 7, of which 6 were waited for; matrix products, arithmetic and copies ran while one was open for 16% of the time, Pallas kernels for 0%

profile of v1, /device:TPU:2, one launch (start us, length us, event | category | flops | bytes accessed | tf_op | source)
XLA Modules:
  0.0 378.5 jit_solution(17971020870842361110)
XLA Ops:
  7.2 0.7 all-gather.3.cloned.1.call-update
  7.9 0.7 all-gather.5.cloned.1.call-update
  8.7 0.7 dynamic_slice.3
  9.4 0.2 convert_reduce_fusion
  9.6 0.7 dynamic-slice_add_fusion
  10.3 0.2 slice_reduce_fusion.3
  10.5 1.0 fusion.46
  11.5 56.1 %all-gather.3.cloned.1.call-done = bf16[256,8192]{1,0:T(8,128)(2,1)} async-done(((bf16[256,1024]{1,0:T(8,128)(2,1)}), bf16[256,8192]{1,0:T(8,128)(2,1)}) %all-gather.3.cloned.1.call-update) | async-done | bytes 4194320 | tf_op jit(solution)/shard_map/all_gather | solution.py:60
  67.6 59.1 %all-gather.5.cloned.1.call-done = bf16[8192,512]{1,0:T(8,128)(2,1)} async-done(((bf16[256,512]{1,0:T(8,128)(2,1)}), bf16[8192,512]{1,0:T(8,128)(2,1)}) %all-gather.5.cloned.1.call-update) | async-done | bytes 8388624 | tf_op jit(solution)/shard_map/all_gather | solution.py:61
  126.7 7.0 %convolution_convert_fusion.4 = bf16[256,512]{1,0:T(8,128)(2,1)S(1)} fusion(bf16[256,8192]{1,0:T(8,128)(2,1)} %all-gather.3.cloned.1.call-done, bf16[8192,512]{1,0:T(8,128)(2,1)} %all-gather.5.cloned.1.call-done), kind=kOutput, calls=%fused_computation.17 | convolution fusion | flops 2147614720 | bytes 12845056 | tf_op jit(solution)/shard_map/dot_general | solution.py:62
  133.7 1.3 select_select_fusion.1
  135.0 4.8 %all-to-all-start.1 = ((bf16[8,1,64,512]{3,2,1,0:T(8,128)(2,1)}), bf16[8,1,64,512]{3,2,1,0:T(8,128)(2,1)S(1)}, u32[]{:S(2)}, u32[]{:S(2)}) async-start(bf16[8,1,64,512]{3,2,1,0:T(8,128)(2,1)} %get-tuple-element.38), calls=%async_computation.1 | async-start | bytes 1048576 | tf_op jit(solution)/shard_map/all_to_all | solution.py:76
  139.8 4.7 %fusion.44 = (bf16[8,1,256,512]{3,2,1,0:T(8,128)(2,1)}, bf16[8,1,256,512]{3,2,1,0:T(8,128)(2,1)}) fusion(bf16[8,2,256,512]{3,2,1,0:T(8,128)(2,1)} %param.9), kind=kLoop, calls=%fused_computation.72 | loop fusion | bytes 8388608 | tf_op jit(solution)/shard_map/slice | solution.py:18
  144.5 2.8 copy.57
  147.3 3.9 %copy.56 = bf16[8,1,256,512]{2,3,0,1:T(8,128)(2,1)} copy(bf16[8,1,256,512]{3,2,1,0:T(8,128)(2,1)} %get-tuple-element.20) | data formatting | bytes 4194304
  151.3 4.8 %all-to-all-start = ((bf16[8,1,64,512]{3,2,1,0:T(8,128)(2,1)}), bf16[8,1,64,512]{3,2,1,0:T(8,128)(2,1)}, u32[]{:S(2)}, u32[]{:S(2)}) async-start(bf16[8,1,64,512]{3,2,1,0:T(8,128)(2,1)} %get-tuple-element.37), calls=%async_computation | async-start | bytes 1048576 | tf_op jit(solution)/shard_map/all_to_all | solution.py:76
  156.1 0.1 reshape_reshape.10
  156.2 1.8 fusion.25
  158.0 7.1 %all-to-all-done = bf16[8,1,64,512]{3,2,1,0:T(8,128)(2,1)} async-done(((bf16[8,1,64,512]{3,2,1,0:T(8,128)(2,1)}), bf16[8,1,64,512]{3,2,1,0:T(8,128)(2,1)}, u32[]{:S(2)}, u32[]{:S(2)}) %all-to-all-start) | async-done | bytes 524320 | tf_op jit(solution)/shard_map/all_to_all | solution.py:76
  165.1 1.2 reshape_reshape.9
  166.2 2.0 fusion.28
  168.3 1.8 fusion.47
  170.1 16.1 %fusion.15 = bf16[8,64,4,128]{3,1,2,0:T(8,128)(2,1)} fusion(bf16[8,256,4,128]{1,3,2,0:T(8,128)(2,1)} %bitcast.89, f32[8,4,64,256]{3,2,1,0:T(8,128)} %fusion.25, f32[8,4,64,256]{3,2,1,0:T(8,128)} %get-tuple-element.48, f32[8,4,64]{2,1,0:T(4,128)S(1)} %get-tuple-element.47), kind=kOutput, calls=%fused_computation.16 | convolution fusion | flops 138152192 | bytes 6823936 | tf_op jit(solution)/shard_map/bhqk,bkhd->bqhd/dot_general | solution.py:38
  186.2 2.2 copy.46
  188.4 2.0 reshape_reshape.11
  190.4 5.5 %all-to-all-start.2 = ((bf16[8,1,64,512]{3,2,1,0:T(8,128)(2,1)}), bf16[8,1,64,512]{3,2,1,0:T(8,128)(2,1)}, u32[]{:S(2)}, u32[]{:S(2)}) async-start(bf16[8,1,64,512]{3,2,1,0:T(8,128)(2,1)} %bitcast.93), calls=%async_computation.2 | async-start | bytes 1048576 | tf_op jit(solution)/shard_map/all_to_all | solution.py:87
  196.0 0.1 broadcast_in_dim.279
  196.2 0.1 broadcast_in_dim.325
  196.3 0.1 broadcast_in_dim.318
  196.5 0.1 broadcast_in_dim.311
  196.7 0.1 broadcast_in_dim.304
  196.8 0.1 broadcast_in_dim.346
  197.0 0.1 broadcast_in_dim.339
  197.1 0.1 broadcast_in_dim.332
  197.2 7.7 %all-to-all-done.2 = bf16[8,1,64,512]{3,2,1,0:T(8,128)(2,1)} async-done(((bf16[8,1,64,512]{3,2,1,0:T(8,128)(2,1)}), bf16[8,1,64,512]{3,2,1,0:T(8,128)(2,1)}, u32[]{:S(2)}, u32[]{:S(2)}) %all-to-all-start.2) | async-done | bytes 524320 | tf_op jit(solution)/shard_map/all_to_all | solution.py:87
  205.0 1.1 slice_bitcast_fusion.7
  206.1 0.3 fusion.36
  206.4 7.8 %fusion.2 = bf16[8192,512]{0,1:T(8,128)(2,1)} fusion(bf16[256,512]{1,0:T(8,128)(2,1)S(1)} %fusion.36, bf16[256,8192]{1,0:T(8,128)(2,1)} %all-gather.3.cloned.1.call-done), kind=kOutput, calls=%fused_computation.3 | convolution fusion | flops 2151677952 | bytes 12845056 | tf_op jit(solution)/shard_map/dot_general | solution.py:105
  214.2 0.2 reduce-scatter.3.cloned.1.call-start
  214.4 7.7 %convolution_convert_fusion.1 = bf16[256,8192]{1,0:T(8,128)(2,1)} fusion(bf16[256,512]{1,0:T(8,128)(2,1)S(1)} %fusion.36, bf16[8192,512]{1,0:T(8,128)(2,1)} %all-gather.5.cloned.1.call-done), kind=kOutput, calls=%fused_computation.4 | convolution fusion | flops 2149580800 | bytes 12845056 | tf_op jit(solution)/shard_map/dot_general | solution.py:98
  222.1 16.7 %convolution_convert_fusion.3 = bf16[8,4,128,256]{3,2,1,0:T(8,128)(2,1)} fusion(f32[8,4,64,256]{3,2,1,0:T(8,128)} %fusion.25, bf16[8,64,4,128]{3,2,1,0:T(4,128)(2,1)S(1)} %reshape_reshape.9, f32[8,4,64,256]{3,2,1,0:T(8,128)} %get-tuple-element.48, f32[8,4,64]{2,1,0:T(4,128)S(1)} %get-tuple-element.47), kind=kOutput, calls=%fused_computation.12 | convolution fusion | flops 138938624 | bytes 6823936 | tf_op jit(solution)/shard_map/bhqk,bqhd->bkhd/dot_general | solution.py:41
  238.8 4.0 %copy.50 = bf16[8,1,256,512]{3,2,1,0:T(8,128)(2,1)} copy(bf16[8,1,256,512]{2,3,0,1:T(8,128)(2,1)} %bitcast.92) | data formatting | bytes 4194304 | tf_op jit(solution)/shard_map/stack | solution.py:44
  242.8 5.3 %convolution_convert_fusion.2 = bf16[8,4,128,256]{3,2,1,0:T(8,128)(2,1)} fusion(bf16[8,64,4,128]{3,2,1,0:T(4,128)(2,1)S(1)} %reshape_reshape.10, f32[8,4,64]{2,1,0:T(4,128)S(1)} %get-tuple-element.47, f32[8,4,64,256]{3,2,1,0:T(8,128)S(1)} %fusion.28, pred[8,256]{1,0:T(8,128)(4,1)S(1)} %broadcast_compare_fusion), kind=kOutput, calls=%fused_computation.11 | convolution fusion | flops 137890048 | bytes 4728832 | tf_op jit(solution)/shard_map/bhqk,bqhd->bkhd/dot_general | solution.py:27
  248.2 4.2 %copy.51 = bf16[8,1,256,512]{3,2,1,0:T(8,128)(2,1)} copy(bf16[8,1,256,512]{2,3,0,1:T(8,128)(2,1)} %bitcast.91) | data formatting | bytes 4194304 | tf_op jit(solution)/shard_map/stack | solution.py:44
  252.4 4.1 %pad_maximum_fusion = bf16[8,2,256,512]{3,2,1,0:T(8,128)(2,1)} fusion(bf16[8,1,256,512]{3,2,1,0:T(8,128)(2,1)} %copy.51, bf16[8,1,256,512]{3,2,1,0:T(8,128)(2,1)S(1)} %copy-done), kind=kLoop, calls=%fused_computation.5 | loop fusion | flops 2097152 | bytes 8388608 | tf_op jit(solution)/shard_map/stack | solution.py:44
  256.5 57.3 %reduce-scatter.5.cloned.1.call-done = bf16[256,512]{0,1:T(8,128)(2,1)} async-done(((bf16[8192,512]{0,1:T(8,128)(2,1)}), bf16[256,512]{0,1:T(8,128)(2,1)}) %reduce-scatter.5.cloned.1.call-update) | async-done | bytes 262160 | tf_op jit(solution)/shard_map/reduce_scatter | solution.py:104
  313.7 1.9 copy.52
  315.6 56.3 %reduce-scatter.3.cloned.1.call-done = bf16[256,1024]{1,0:T(8,128)(2,1)} async-done(((bf16[256,8192]{1,0:T(8,128)(2,1)}), bf16[256,1024]{1,0:T(8,128)(2,1)}) %reduce-scatter.3.cloned.1.call-update) | async-done | bytes 524304 | tf_op jit(solution)/shard_map/reduce_scatter | solution.py:101
  (22 shorter events, 0.7 us)
Async XLA Ops:
  7.2 60.4 %all-gather.3.cloned.1.call-start = ((), (), s32[]{:S(2)}) async-start(), calls=%async_computation.5 | async-start | bytes 4718592 | tf_op jit(solution)/shard_map/all_gather | solution.py:60
  7.9 118.8 %all-gather.5.cloned.1.call-start = ((), (), s32[]{:S(2)}) async-start(), calls=%async_computation.6 | async-start | bytes 8650752 | tf_op jit(solution)/shard_map/all_gather | solution.py:61
  135.0 16.3 %all-to-all-start.1 = ((bf16[8,1,64,512]{3,2,1,0:T(8,128)(2,1)}), bf16[8,1,64,512]{3,2,1,0:T(8,128)(2,1)S(1)}, u32[]{:S(2)}, u32[]{:S(2)}) async-start(bf16[8,1,64,512]{3,2,1,0:T(8,128)(2,1)} %get-tuple-element.38), calls=%async_computation.1 | async-start | bytes 1048576 | tf_op jit(solution)/shard_map/all_to_all | solution.py:76
  147.3 8.7 %copy-start.1 = (s32[8,256]{1,0:T(8,128)S(1)}, s32[8,256]{1,0:T(8,128)}, u32[]{:S(2)}) copy-start(s32[8,256]{1,0:T(8,128)} %param.10) | copy-start | bytes 24580
  151.3 13.8 %all-to-all-start = ((bf16[8,1,64,512]{3,2,1,0:T(8,128)(2,1)}), bf16[8,1,64,512]{3,2,1,0:T(8,128)(2,1)}, u32[]{:S(2)}, u32[]{:S(2)}) async-start(bf16[8,1,64,512]{3,2,1,0:T(8,128)(2,1)} %get-tuple-element.37), calls=%async_computation | async-start | bytes 1048576 | tf_op jit(solution)/shard_map/all_to_all | solution.py:76
  190.4 14.5 %all-to-all-start.2 = ((bf16[8,1,64,512]{3,2,1,0:T(8,128)(2,1)}), bf16[8,1,64,512]{3,2,1,0:T(8,128)(2,1)}, u32[]{:S(2)}, u32[]{:S(2)}) async-start(bf16[8,1,64,512]{3,2,1,0:T(8,128)(2,1)} %bitcast.93), calls=%async_computation.2 | async-start | bytes 1048576 | tf_op jit(solution)/shard_map/all_to_all | solution.py:87
  195.9 117.8 %reduce-scatter.5.cloned.1.call-start = ((), (), s32[]{:S(2)}) async-start(), calls=%async_computation.8 | async-start | bytes 8650752 | tf_op jit(solution)/shard_map/reduce_scatter | solution.py:104
  214.2 157.7 %reduce-scatter.3.cloned.1.call-start = ((), (), s32[]{:S(2)}) async-start(), calls=%async_computation.7 | async-start | bytes 4718592 | tf_op jit(solution)/shard_map/reduce_scatter | solution.py:101
  248.2 4.2 %copy-start = (bf16[8,1,256,512]{3,2,1,0:T(8,128)(2,1)S(1)}, bf16[8,1,256,512]{3,2,1,0:T(8,128)(2,1)}, u32[]{:S(2)}) copy-start(bf16[8,1,256,512]{3,2,1,0:T(8,128)(2,1)} %copy.50) | copy-start | bytes 6291460
Sparse Core Ops, SparseCore 0:
  9.8 57.7 all-gather.2
  70.2 56.4 all-gather.4
  214.3 99.3 reduce-scatter.4
  316.9 55.0 reduce-scatter.2

commit v2 on v1

v2 whole, which is shorter than its diff:
```python
import functools

import jax
import jax.numpy as jnp
from jax import lax
from jax.experimental import pallas as pl
from jax.experimental.pallas import tpu as pltpu
from jax.sharding import PartitionSpec as P

HD = 128
SPAN = 64
KEYS = 256
MESH = pl.DeviceIdType.MESH
BF = jnp.bfloat16
F32 = jnp.float32
NN = (((1,), (0,)), ((), ()))
NT = (((1,), (1,)), ((), ()))
TN = (((0,), (0,)), ((), ()))


def dot(a, b, dims):
    return lax.dot_general(a, b, dims, preferred_element_type=F32)


def kernel(
    act_ref, w_ref, g_ref, kv_ref, ids_ref, owner_ref,
    act_out, w_out, kv_out,
    act_full, act_t, w_full, kv_v, kvg, g_v, q_acc,
    q_send, q_recv, g_send, g_recv, dq_send, dq_recv, dq_v,
    z_send, z_recv, sib_send, red, p1q, p1h, s1h, f1, f1b, s2h, p2q, p2h,
    send_sems, recv_sems, dq_ssem, dq_rsem, loc_sems, kv_sems,
):
    s = lax.axis_index("seq")
    z = lax.axis_index("tensor")
    y = lax.axis_index("dp")
    x = s // 2
    core = s % 2
    TOK = g_v.shape[0]
    HALF = TOK // 2
    QUART = HALF // 2
    BLK = w_ref.shape[0]

    def mod4(v):
        return lax.rem(v + 4, 4)

    def mod8(v):
        return lax.rem(v + 8, 8)

    z_dev = {1: {"tensor": mod8(z + 1)}, -1: {"tensor": mod8(z - 1)}}
    x_dev = {1: {"seq": mod4(x + 1) * 2 + core}, -1: {"seq": mod4(x - 1) * 2 + core}}
    y_dev = {1: {"dp": mod4(y + 1)}, -1: {"dp": mod4(y - 1)}}
    sib = {"seq": s + 1 - 2 * core}

    barrier = pltpu.get_barrier_semaphore()
    partners = [z_dev[1], z_dev[-1], y_dev[1], y_dev[-1]]
    partners += [{"seq": mod8(s + k)} for k in range(1, 8)]
    for dev in partners:
        pl.semaphore_signal(barrier, inc=1, device_id=dev, device_id_type=MESH)

    loads = []

    def load(src, dst):
        d = pltpu.make_async_copy(src, dst, loc_sems.at[len(loads)])
        d.start()
        loads.append(d)
        return d

    own_rows = pl.ds(pl.multiple_of(y * BLK, BLK), BLK)
    ld_act = load(act_ref, act_full.at[z])
    ld_w = load(w_ref, w_full.at[s, own_rows])
    ld_g = load(g_ref, g_v)
    ld_kv = load(kv_ref, kv_v)
    pl.semaphore_wait(barrier, len(partners))

    sends = []

    def push(src, dst, dev):
        n = len(sends)
        d = pltpu.make_async_remote_copy(
            src_ref=src, dst_ref=dst, send_sem=send_sems.at[n], recv_sem=recv_sems.at[n],
            device_id=dev, device_id_type=MESH,
        )
        d.start()
        sends.append(d)
        return d

    def act_rows(chunk):
        return pl.ds(chunk * HALF, HALF)

    zf = {}

    def z_first(chunk):
        for d in (1, -1):
            zf[d, 0, chunk] = push(
                act_ref.at[act_rows(chunk)], act_full.at[z, act_rows(chunk)], z_dev[d]
            )

    def z_fwd(t, chunk):
        for d in (1, -1):
            if (d, t, chunk) not in zf:
                continue
            zf[d, t, chunk].wait_recv()
            last = t == 3 or (t == 2 and chunk != (0 if d == 1 else 1))
            if not last:
                ref = act_full.at[mod8(z - d * (t + 1)), act_rows(chunk)]
                zf[d, t + 1, chunk] = push(ref, ref, z_dev[d])

    def w_ref_at(h, k1, k2, off, n, c=None):
        dx, dy = (k1, k2) if h == 0 else (k2, k1)
        seq = mod4(x + dx) * 2 + (core if c is None else c)
        return w_full.at[seq, pl.ds(pl.multiple_of(mod4(y + dy) * BLK + h * HALF + off, QUART), n)]

    ax = {0: (x_dev, y_dev), 1: (y_dev, x_dev)}
    sib_w = []

    def to_sib(h, k1, k2):
        ref = w_ref_at(h, k1, k2, 0, HALF)
        sib_w.append(push(ref, ref, sib))

    wp1, wp1b, wp2, wp2b = {}, {}, {}, {}

    def w_start_p1(h):
        src = w_ref.at[pl.ds(h * HALF, HALF)]
        for d in (1, -1):
            wp1[h, d] = push(src, w_ref_at(h, 0, 0, 0, HALF), ax[h][0][d])

    def w_start_p2(h):
        src = w_ref.at[pl.ds(h * HALF, HALF)]
        for d in (1, -1):
            wp2[h, 0, d] = push(src, w_ref_at(h, 0, 0, 0, HALF), ax[h][1][d])

    def w_p2_send(h, k):
        ref = w_ref_at(h, k, 0, 0, HALF)
        for d in (1, -1):
            wp2[h, k, d] = push(ref, ref, ax[h][1][d])

    def w_p1_hop1(h):
        for d in (1, -1):
            wp1[h, d].wait_recv()
            ref = w_ref_at(h, -d, 0, 0 if d == 1 else QUART, QUART)
            wp1b[h, d] = push(ref, ref, ax[h][0][d])
            w_p2_send(h, -d)
            to_sib(h, -d, 0)

    def w_p1_hop2(h):
        for d in (1, -1):
            wp1b[h, d].wait_recv()
        w_p2_send(h, 2)
        to_sib(h, 2, 0)

    def w_p2_hop1(h, k):
        for d in (1, -1):
            wp2[h, k, d].wait_recv()
            ref = w_ref_at(h, k, -d, 0 if d == 1 else QUART, QUART)
            wp2b[h, k, d] = push(ref, ref, ax[h][1][d])
            to_sib(h, k, -d)

    def w_p2_hop2(h, k):
        for d in (1, -1):
            wp2b[h, k, d].wait_recv()
        to_sib(h, k, 2)

    both = (0, 1)
    z_first(0)
    for h in both:
        w_start_p1(h)
    for h in both:
        w_start_p2(h)
    z_first(1)
    sib_w.append(push(w_ref, w_full.at[s, own_rows], sib))

    block = s * 4 + y
    names = [owner_ref[block * 4 + c] for c in range(4)]

    def to_slots(rows_ref, send, recv):
        for k in range(8):
            o = mod8(s + k)
            v = jnp.zeros((SPAN, rows_ref.shape[1]), BF)
            for c in range(4):
                v = jnp.where(names[c] == o, rows_ref[c * SPAN:(c + 1) * SPAN, :].astype(BF), v)
            if k == 0:
                recv[s] = v
            else:
                send[k] = v

    ld_g.wait()
    to_slots(g_v, g_send, g_recv)
    ld_act.wait()
    ld_w.wait()

    for h in both:
        w_p1_hop1(h)
    z_fwd(0, 0)
    for h in both:
        w_p2_hop1(h, 0)
    for h in both:
        w_p1_hop2(h)
    g_copies = {
        k: push(g_send.at[k], g_recv.at[s], {"seq": mod8(s + k)}) for k in range(1, 8)
    }
    z_fwd(0, 1)

    def turn(slot):
        act_t[slot] = jnp.transpose(act_full[slot])

    turn(z)
    for h in both:
        w_p2_hop1(h, -1)
        w_p2_hop1(h, 1)
    z_fwd(1, 0)
    for h in both:
        w_p2_hop1(h, 2)
    z_fwd(1, 1)
    for h in both:
        w_p2_hop2(h, 0)
    turn(mod8(z + 1))
    turn(mod8(z - 1))
    for h in both:
        w_p2_hop2(h, -1)
        w_p2_hop2(h, 1)
    z_fwd(2, 0)
    for h in both:
        w_p2_hop2(h, 2)
    for d in sib_w:
        d.wait_recv()

    def add_q(slot):
        q_acc[...] += dot(act_full[slot], w_full[slot], NN)

    q_acc[...] = jnp.zeros_like(q_acc)
    add_q(z)
    for k in (1, -1):
        add_q(mod8(z + k))
    z_fwd(2, 1)
    for k in (2, -2):
        add_q(mod8(z + k))
        turn(mod8(z + k))
    for k in (3, -3):
        add_q(mod8(z + k))
        turn(mod8(z + k))
    ld_kv.wait()
    z_fwd(3, 0)
    z_fwd(3, 1)
    add_q(mod8(z + 4))

    to_slots(q_acc, q_send, q_recv)
    q_copies = {
        k: push(q_send.at[k], q_recv.at[s], {"seq": mod8(s + k)}) for k in range(1, 8)
    }
    turn(mod8(z + 4))
    for k in range(1, 8):
        g_copies[k].wait_recv()
    for k in range(1, 8):
        q_copies[k].wait_recv()
    scale = HD ** (-0.5)
    heads = g_v.shape[1] // HD

    def dq_copy(k):
        j = mod8(s - k)
        return pltpu.make_async_remote_copy(
            src_ref=dq_send.at[j], dst_ref=dq_recv.at[s], send_sem=dq_ssem.at[k],
            recv_sem=dq_rsem.at[k], device_id={"seq": j}, device_id_type=MESH,
        )

    def kv_copy(k):
        j = mod8(s - k)
        return pltpu.make_async_copy(kvg.at[j], kv_out.at[j], kv_sems.at[k])

    def slot_step(i, carry):
        k = 7 - i
        j = mod8(s - k)
        live = ids_ref[pl.ds(j, 1), :] != 0
        for h in range(heads):
            cols = slice(h * HD, (h + 1) * HD)
            q = q_recv[j, :, cols]
            g = g_recv[j, :, cols]
            key = kv_v[j, 0, :, cols]
            val = kv_v[j, 1, :, cols]
            sc = jnp.where(live, dot(q, key, NT) * scale, -1e30)
            ex = jnp.exp(sc - jnp.max(sc, axis=1, keepdims=True))
            probs = ex / jnp.sum(ex, axis=1, keepdims=True)
            pg = dot(g, val, NT)
            center = jnp.sum(probs * pg, axis=1, keepdims=True)
            sg = (probs * (pg - center) * scale).astype(BF)
            dq_send[j, :, cols] = dot(sg, key, NN).astype(BF)
            kvg[j, 0, :, cols] = dot(sg, q, TN).astype(BF)
            kvg[j, 1, :, cols] = dot(probs.astype(BF), g, TN).astype(BF)

        @pl.when(k > 0)
        def _():
            dq_copy(k).start()

        kv_copy(k).start()
        return carry

    lax.fori_loop(0, 8, slot_step, 0)
    dq_recv[s] = dq_send[s]
    for k in range(1, 8):
        dq_copy(k).wait_recv()
    for c in range(4):
        v = jnp.zeros((SPAN, g_v.shape[1]), BF)
        for o in range(8):
            v = jnp.where(names[c] == o, dq_recv[o], v)
        dq_v[c * SPAN:(c + 1) * SPAN, :] = v

    def part_act(dest, chunk):
        return dot(dq_v[chunk * HALF:(chunk + 1) * HALF, :], w_full[mod8(dest)], NT)

    zb = {}

    def z_push(d, dist, chunk, value):
        n = len(zb)
        z_send[n] = value.astype(BF)
        zb[d, dist, chunk] = (push(z_send.at[n], z_recv.at[n], z_dev[d]), n)

    def z_got(d, dist, chunk):
        copy, n = zb[d, dist, chunk]
        copy.wait_recv()
        return z_recv[n].astype(F32)

    def z_add(dist, chunk):
        for d in (1, -1):
            ch = chunk if d == 1 else 1 - chunk
            got = z_got(d, dist, ch)
            z_push(d, dist - 1, ch, got + part_act(z + d * (dist - 1), ch))

    z_push(1, 4, 0, part_act(z + 4, 0))
    z_push(-1, 4, 1, part_act(z + 4, 1))
    z_push(1, 3, 1, part_act(z + 3, 1))
    z_push(-1, 3, 0, part_act(z - 3, 0))

    order = [(kx, 2) for kx in (2, 1, 3, 0)] + [(2, ky) for ky in (1, 3, 0)]
    order += [(kx, ky) for kx in (1, 3, 0) for ky in (1, 3, 0)]

    def part_w(kx, ky, c):
        rows = pl.ds(pl.multiple_of(mod4(y + ky) * BLK, BLK), BLK)
        return dot(act_t[mod4(x + kx) * 2 + c, rows], dq_v[...], NN)

    sib_d = {}
    for n, (kx, ky) in enumerate(order):
        sib_send[n] = part_w(kx, ky, 1 - core).astype(BF)
        sib_d[kx, ky] = (push(sib_send.at[n], red.at[n], sib), n)
    z_add(4, 0)

    def red_at(h, kf, ku, off, n):
        kx, ky = (kf, ku) if h == 0 else (ku, kf)
        return red.at[order.index((kx % 4, ky % 4)), pl.ds(h * HALF + off, n)]

    def pair_sum(kx, ky):
        copy, n = sib_d[kx, ky]
        copy.wait_recv()
        red[n] = (red[n].astype(F32) + part_w(kx, ky, core)).astype(BF)

    first_ax = {0: y_dev, 1: x_dev}
    second_ax = {0: x_dev, 1: y_dev}
    c1q, c1h, c2q, c2h = {}, {}, {}, {}

    def quarter1(h, kf):
        c1q[h, 1, kf] = push(red_at(h, kf, 2, 0, QUART), p1q.at[h, 0, kf], first_ax[h][1])
        c1q[h, -1, kf] = push(red_at(h, kf, 2, QUART, QUART), p1q.at[h, 1, kf], first_ax[h][-1])

    def half1(h, kf):
        for e, d in enumerate((1, -1)):
            c1q[h, d, kf].wait_recv()
            src = red_at(h, kf, d, 0, HALF)
            got = p1q[h, e, kf].astype(F32)
            lo = src[:QUART].astype(F32)
            hi = src[QUART:].astype(F32)
            lo, hi = (lo + got, hi) if d == 1 else (lo, hi + got)
            s1h[h, e, kf, :QUART] = lo.astype(BF)
            s1h[h, e, kf, QUART:] = hi.astype(BF)
            c1h[h, d, kf] = push(s1h.at[h, e, kf], p1h.at[h, e, kf], first_ax[h][d])

    def final1(h, kf):
        for d in (1, -1):
            c1h[h, d, kf].wait_recv()
        v = red_at(h, kf, 0, 0, HALF)[...].astype(F32)
        v = v + p1h[h, 0, kf].astype(F32) + p1h[h, 1, kf].astype(F32)
        if kf == 2:
            f1b[h] = v.astype(BF)
            c2q[h, 1] = push(f1b.at[h, pl.ds(0, QUART)], p2q.at[h, 0], second_ax[h][1])
            c2q[h, -1] = push(f1b.at[h, pl.ds(QUART, QUART)], p2q.at[h, 1], second_ax[h][-1])
        else:
            f1[h, kf] = v

    def half2(h):
        for e, d in enumerate((1, -1)):
            c2q[h, d].wait_recv()
            got = p2q[h, e].astype(F32)
            lo = f1[h, d % 4, :QUART]
            hi = f1[h, d % 4, QUART:]
            lo, hi = (lo + got, hi) if d == 1 else (lo, hi + got)
            s2h[h, e, :QUART] = lo.astype(BF)
            s2h[h, e, QUART:] = hi.astype(BF)
            c2h[h, d] = push(s2h.at[h, e], p2h.at[h, e], second_ax[h][d])

    def final2(h):
        for d in (1, -1):
            c2h[h, d].wait_recv()
        w_out[h * HALF:(h + 1) * HALF, :] = (
            f1[h, 0] + p2h[h, 0].astype(F32) + p2h[h, 1].astype(F32)
        )

    for kx, ky in order[:4]:
        pair_sum(kx, ky)
        quarter1(0, kx)
    for ky in (2, 1, 3, 0):
        if ky != 2:
            pair_sum(2, ky)
        quarter1(1, ky)
    z_add(3, 1)
    for kx, ky in order[7:]:
        pair_sum(kx, ky)
    for kf in (2, 1, 3, 0):
        for h in both:
            half1(h, kf)
    z_add(3, 0)
    for h in both:
        final1(h, 2)
    z_add(2, 1)
    for kf in (1, 3):
        for h in both:
            final1(h, kf)
    for h in both:
        half2(h)
    for h in both:
        final1(h, 0)
    z_add(2, 0)
    for h in both:
        final2(h)
    for chunk in (1, 0):
        own = part_act(z, chunk)
        got = z_got(1, 1, chunk) + z_got(-1, 1, chunk)
        act_out[chunk * HALF:(chunk + 1) * HALF, :] = (own + got).astype(BF)

    for d in sends:
        d.wait_send()
    for k in range(8):
        if k:
            dq_copy(k).wait_send()
        kv_copy(k).wait()


def on_device(span_act, q_weight, out_grad, neighbour_kv, neighbour_ids, owner):
    tok, width = out_grad.shape
    dcol = span_act.shape[1]
    half, quart = tok // 2, tok // 4
    any_spec = pl.BlockSpec(memory_space=pl.ANY)
    vmem = pl.BlockSpec(memory_space=pltpu.VMEM)

    def bf(*shape):
        return pltpu.VMEM(shape, BF)

    def f32(*shape):
        return pltpu.VMEM(shape, F32)

    return pl.pallas_call(
        kernel,
        out_shape=(
            jax.ShapeDtypeStruct((tok, dcol), BF),
            jax.ShapeDtypeStruct((q_weight.shape[0], width), F32),
            jax.ShapeDtypeStruct(neighbour_kv.shape, BF),
        ),
        in_specs=[any_spec, any_spec, any_spec, any_spec, vmem,
                  pl.BlockSpec(memory_space=pltpu.SMEM)],
        out_specs=(vmem, vmem, any_spec),
        scratch_shapes=[
            bf(8, tok, dcol), bf(8, dcol, tok), bf(8, dcol, width),
            bf(*neighbour_kv.shape), bf(*neighbour_kv.shape), bf(tok, width), f32(tok, width),
            bf(8, SPAN, width), bf(8, SPAN, width), bf(8, SPAN, width), bf(8, SPAN, width),
            bf(8, SPAN, width), bf(8, SPAN, width), bf(tok, width),
            bf(14, half, dcol), bf(14, half, dcol),
            bf(16, tok, width), bf(16, tok, width),
            bf(2, 2, 4, quart, width), bf(2, 2, 4, half, width), bf(2, 2, 4, half, width),
            f32(2, 4, half, width), bf(2, half, width), bf(2, 2, half, width),
            bf(2, 2, quart, width), bf(2, 2, half, width),
            pltpu.SemaphoreType.DMA((180,)), pltpu.SemaphoreType.DMA((180,)),
            pltpu.SemaphoreType.DMA((8,)), pltpu.SemaphoreType.DMA((8,)),
            pltpu.SemaphoreType.DMA((4,)), pltpu.SemaphoreType.DMA((8,)),
        ],
        compiler_params=pltpu.CompilerParams(
            collective_id=0, has_side_effects=True, vmem_limit_bytes=60 * 1024 * 1024
        ),
        cost_estimate=pl.CostEstimate(
            flops=8 * 10**9, bytes_accessed=16 * 2**20, transcendentals=600000
        ),
    )(span_act, q_weight, out_grad, neighbour_kv, neighbour_ids, owner)


def solution(mesh):
    in_specs = (
        P(("seq", "dp"), "tensor"),
        P(("seq", "dp"), "tensor"),
        P(("seq", "dp"), "tensor"),
        P(("seq", "dp"), None, None, "tensor"),
        P(("seq", "dp"), None),
        P(),
    )
    out_specs = (
        P(("seq", "dp"), "tensor"),
        P(("seq", "dp"), "tensor"),
        P(("seq", "dp"), None, None, "tensor"),
    )
    return jax.shard_map(
        on_device, mesh=mesh, in_specs=in_specs, out_specs=out_specs, check_vma=False
    )
```

time: 380 us -> 133 us (0.35)
  waiting for transfers between devices: 245 us -> 0 us
  Pallas kernels: 0 us -> 122 us
  matrix products: 64.3 us -> 0 us
  local copies, waits for them, and re-layouts: 31.4 us -> 8.31 us
  starting transfers between devices: 15.4 us -> 0 us
  between operations: 13.9 us -> 0.64 us
  other arithmetic: 8.5 us -> 0 us
    pallas_call x0 -> x1, Pallas kernels: none -> 122 us  [on_device(): pl.pallas_call(kernel, out_shape=(jax.ShapeDtypeStruct((tok, dcol), BF),...]
    all_gather x2 -> x0, waiting for transfers between devices: 115 us -> none  [the longest x1 59.1 us: on_device(): weights = lax.all_gather(q_weight, ('seq', 'dp'), axis=0, tiled=True)]
    reduce_scatter x2 -> x0, waiting for transfers between devices: 114 us -> none  [the longest x1 57.3 us: on_device(): lax.psum_scatter(lax.dot_general(whole, flat_grad, (((0,), (0,)), ((), ()...]
    dot_general x8 -> x0, matrix products: 64.3 us -> none  [the longest x1 16.7 us: attend_back(): jnp.einsum('bhqk,bqhd->bkhd', score_grad, query_heads, preferred_element_...]
    all_to_all x3 -> x0, starting transfers between devices: 15.1 us -> none  [the longest x2 9.61 us: to_owner(): lax.all_to_all(slots.reshape(seq_count, pairs, SPAN, width), 'seq', split...]
    all_to_all x3 -> x0, waiting for transfers between devices: 14.8 us -> none  [the longest x1 7.72 us: on_device(): lax.all_to_all(slot_grad.reshape(seq_count, pairs, SPAN, width), 'seq', s...]
    another operation x5 -> x0, local copies, waits for them, and re-layouts: 11.5 us -> none  [the longest x2 8.19 us: attend_back(): jnp.stack([key_grad.astype(jnp.bfloat16), value_grad.astype(jnp.bfloat16)...]
    slice x4 -> x0, local copies, waits for them, and re-layouts: 5.87 us -> none  [the longest x1 4.68 us: attend_back(): value_heads = pair_kv[:, 1].reshape(slots, -1, heads, HD)]
  transfers between devices with their start and end apart: 7 -> 0, of which waited for: 6 -> 0; matrix products, arithmetic and copies ran while one was open for 16% -> 0% of each run, Pallas kernels for 0% -> 0%
where the time goes in v2:
time: 133 us; the launch traced here: 131 us
  Pallas kernels  122 us (92%)
  local copies, waits for them, and re-layouts  8.31 us (6%)
    pallas_call x1, Pallas kernels, on_device(): pl.pallas_call(kernel, out_shape=(jax.ShapeDtypeStruct((tok, dcol), BF),...  122 us
    unnamed x3, local copies, waits for them, and re-layouts  8.31 us

profile of v2, /device:TPU:2, one launch (start us, length us, event | category | flops | bytes accessed | tf_op | source)
XLA Modules:
  0.0 130.7 jit_solution(11325868377569284310)
XLA Ops:
  0.6 121.8 %shard_map.85 = (bf16[256,1024]{1,0:T(8,128)(2,1)}, f32[256,512]{1,0:T(8,128)}, bf16[8,2,256,512]{3,2,1,0:T(8,128)(2,1)}) custom-call(bf16[256,1024]{1,0:T(8,128)(2,1)} %act_ref.1, bf16[256,512]{1,0:T(8,128)(2,1)} %w_ref.1, bf16[256,512]{1,0:T(8,128)(2,1)} %g_ref.1, bf16[8,2,256,512]{3,2,1,0:T(8,128)(2,1)} %kv_ref.1, s32[8,256]{1,0:T(8,128)} %ids_ref.1, ...), custom_call_target="tpu_custom_call" | custom-call | flops 8000000000 | bytes 16777216 | tf_op jit(solution)/shard_map/pallas_call | solution.py:457
  122.4 1.9 %copy.12 = bf16[256,1024]{1,0:T(8,128)(2,1)} copy(bf16[256,1024]{1,0:T(8,128)(2,1)} %get-tuple-element.6) | data formatting | bytes 1048576
  124.3 1.9 %copy.13 = f32[256,512]{1,0:T(8,128)} copy(f32[256,512]{1,0:T(8,128)} %get-tuple-element.7) | data formatting | bytes 1048576
  126.2 4.6 %copy.14 = bf16[8,2,256,512]{3,2,1,0:T(8,128)(2,1)} copy(bf16[8,2,256,512]{3,2,1,0:T(8,128)(2,1)} %get-tuple-element.8) | data formatting | bytes 8388608

commit v3 on v2

v3 whole, which is shorter than its diff:
```python
import functools

import jax
import jax.numpy as jnp
from jax import lax
from jax.experimental import pallas as pl
from jax.experimental.pallas import tpu as pltpu
from jax.sharding import PartitionSpec as P

HD = 128
SPAN = 64
KEYS = 256
MESH = pl.DeviceIdType.MESH
BF = jnp.bfloat16
F32 = jnp.float32
NN = (((1,), (0,)), ((), ()))
NT = (((1,), (1,)), ((), ()))
TN = (((0,), (0,)), ((), ()))


def dot(a, b, dims):
    return lax.dot_general(a, b, dims, preferred_element_type=F32)


def kernel(
    act_ref, w_ref, g_ref, kv_ref, ids_ref, owner_ref,
    act_o, w_o, kv_out,
    act_out, w_out,
    act_full, act_t, w_full, kv_v, pg_v, probs_v, sg_v, g_v, q_acc, q_v,
    q_send, q_recv, g_send, g_recv, dq_send, dq_recv, dq_v,
    z_send, z_recv, pend, sib_send, red, p1q, p1h, s1h, f1, f1b, s2h, p2q, p2h,
    send_sems, recv_sems, g_ssem, g_rsem, q_ssem, q_rsem, dq_ssem, dq_rsem, loc_sems, kv_sems, out_sems,
):
    s = lax.axis_index("seq")
    z = lax.axis_index("tensor")
    y = lax.axis_index("dp")
    x = s // 2
    core = s % 2
    TOK = g_v.shape[0]
    HALF = TOK // 2
    QUART = HALF // 2
    BLK = w_ref.shape[0]

    def mod4(v):
        return lax.rem(v + 4, 4)

    def mod8(v):
        return lax.rem(v + 8, 8)

    z_dev = {1: {"tensor": mod8(z + 1)}, -1: {"tensor": mod8(z - 1)}}
    x_dev = {1: {"seq": mod4(x + 1) * 2 + core}, -1: {"seq": mod4(x - 1) * 2 + core}}
    y_dev = {1: {"dp": mod4(y + 1)}, -1: {"dp": mod4(y - 1)}}
    sib = {"seq": s + 1 - 2 * core}

    barrier = pltpu.get_barrier_semaphore()
    partners = [z_dev[1], z_dev[-1], y_dev[1], y_dev[-1]]
    partners += [{"seq": mod8(s + k)} for k in range(1, 8)]
    for dev in partners:
        pl.semaphore_signal(barrier, inc=1, device_id=dev, device_id_type=MESH)

    loads = []

    def load(src, dst):
        d = pltpu.make_async_copy(src, dst, loc_sems.at[len(loads)])
        d.start()
        loads.append(d)
        return d

    own_rows = pl.ds(pl.multiple_of(y * BLK, BLK), BLK)
    PART = SPAN // 2
    ld_act = [
        load(
            act_ref.at[pl.ds(c * SPAN + ch * PART, PART)],
            act_full.at[z, pl.ds(ch * HALF + c * PART, PART)],
        )
        for ch in (0, 1) for c in range(4)
    ]
    ld_w = load(w_ref, w_full.at[s, own_rows])
    ld_g = load(g_ref, g_v)
    ld_kv = load(kv_ref, kv_v)
    pl.semaphore_wait(barrier, len(partners))

    sends = []
    used = []

    def push(src, dst, dev):
        n = len(used)
        used.append(n)
        d = pltpu.make_async_remote_copy(
            src_ref=src, dst_ref=dst, send_sem=send_sems.at[n], recv_sem=recv_sems.at[n],
            device_id=dev, device_id_type=MESH,
        )
        d.start()
        sends.append(d)
        return d

    def act_rows(ch, sub):
        return pl.ds(ch * HALF + sub * QUART, QUART)

    zf = {}

    def z_first(ch):
        for sub in (0, 1):
            if ch == 0:
                for d in (1, -1):
                    zf[d, 0, ch, sub] = [
                        push(
                            act_ref.at[pl.ds(c * SPAN, PART)],
                            act_full.at[z, pl.ds(c * PART, PART)], z_dev[d],
                        )
                        for c in (2 * sub, 2 * sub + 1)
                    ]
            else:
                ref = act_full.at[z, act_rows(ch, sub)]
                for d in (1, -1):
                    zf[d, 0, ch, sub] = [push(ref, ref, z_dev[d])]

    def z_fwd(ch, t, sub):
        for d in (1, -1):
            if (d, t, ch, sub) not in zf:
                continue
            for copy in zf[d, t, ch, sub]:
                copy.wait_recv()
            if t < 2 or (t == 2 and sub == (0 if d == 1 else 1)):
                ref = act_full.at[mod8(z - d * (t + 1)), act_rows(ch, sub)]
                zf[d, t + 1, ch, sub] = [push(ref, ref, z_dev[d])]

    def w_ref_at(h, k1, k2, off, n, c=None):
        dx, dy = (k1, k2) if h == 0 else (k2, k1)
        seq = mod4(x + dx) * 2 + (core if c is None else c)
        return w_full.at[seq, pl.ds(pl.multiple_of(mod4(y + dy) * BLK + h * HALF + off, QUART), n)]

    ax = {0: (x_dev, y_dev), 1: (y_dev, x_dev)}
    sib_w = []

    def to_sib(h, k1, k2):
        ref = w_ref_at(h, k1, k2, 0, HALF)
        sib_w.append(push(ref, ref, sib))

    wp1, wp1b, wp2, wp2b = {}, {}, {}, {}

    def w_start_p1(h):
        src = w_ref.at[pl.ds(h * HALF, HALF)]
        for d in (1, -1):
            wp1[h, d] = push(src, w_ref_at(h, 0, 0, 0, HALF), ax[h][0][d])

    def w_start_p2(h):
        src = w_ref.at[pl.ds(h * HALF, HALF)]
        for d in (1, -1):
            wp2[h, 0, d] = push(src, w_ref_at(h, 0, 0, 0, HALF), ax[h][1][d])

    def w_p2_send(h, k):
        ref = w_ref_at(h, k, 0, 0, HALF)
        for d in (1, -1):
            wp2[h, k, d] = push(ref, ref, ax[h][1][d])

    def w_p1_hop1(h):
        for d in (1, -1):
            wp1[h, d].wait_recv()
            ref = w_ref_at(h, -d, 0, 0 if d == 1 else QUART, QUART)
            wp1b[h, d] = push(ref, ref, ax[h][0][d])
            w_p2_send(h, -d)
            to_sib(h, -d, 0)

    def w_p1_hop2(h):
        for d in (1, -1):
            wp1b[h, d].wait_recv()
        w_p2_send(h, 2)
        to_sib(h, 2, 0)

    def w_p2_hop1(h, k):
        for d in (1, -1):
            wp2[h, k, d].wait_recv()
            ref = w_ref_at(h, k, -d, 0 if d == 1 else QUART, QUART)
            wp2b[h, k, d] = push(ref, ref, ax[h][1][d])
            to_sib(h, k, -d)

    def w_p2_hop2(h, k):
        for d in (1, -1):
            wp2b[h, k, d].wait_recv()
        to_sib(h, k, 2)

    both = (0, 1)
    z_first(0)
    for h in both:
        w_start_p1(h)
    for h in both:
        w_start_p2(h)
    for d in ld_act:
        d.wait()
    z_first(1)
    sib_w.append(push(w_ref, w_full.at[s, own_rows], sib))

    block = s * 4 + y
    names = [owner_ref[block * 4 + c] for c in range(4)]

    def peer(dx, dc):
        return mod4(x + dx) * 2 + lax.rem(core + dc, 2)

    def owner_copy(send, recv, ssem, rsem, k, dev):
        return pltpu.make_async_remote_copy(
            src_ref=send, dst_ref=recv, send_sem=ssem.at[k], recv_sem=rsem.at[k],
            device_id={"seq": dev}, device_id_type=MESH,
        )

    def picked(rows, o):
        v = jnp.zeros(rows[0].shape, BF)
        for c in range(4):
            v = jnp.where(names[c] == o, rows[c], v)
        return v

    def g_pick():
        rows = [g_v[c * SPAN:(c + 1) * SPAN, :] for c in range(4)]
        for dx in range(4):
            for dc in (0, 1):
                o, k = peer(dx, dc), dx * 2 + dc
                if k == 0:
                    g_recv[s] = picked(rows, o)
                else:
                    g_send[k] = picked(rows, o)

    def g_out():
        copies = {}
        for k in (4, 5, 2, 3, 6, 7, 1):
            o = peer(k // 2, k % 2)
            copies[k] = owner_copy(g_send.at[k], g_recv.at[s], g_ssem, g_rsem, k, o)
            copies[k].start()
            sends.append(copies[k])
        return copies

    def q_out(ch):
        rows = [
            q_acc[ch * HALF + c * PART:ch * HALF + (c + 1) * PART, :].astype(BF) for c in range(4)
        ]
        for dx in (2, 1, 3, 0):
            for dc in (0, 1):
                o, k = peer(dx, dc), dx * 2 + dc
                if k == 0:
                    q_recv[s, ch * PART:(ch + 1) * PART, :] = picked(rows, o)
                else:
                    q_send[ch, k] = picked(rows, o)
                    copy = owner_copy(
                        q_send.at[ch, k], q_recv.at[s, pl.ds(ch * PART, PART)],
                        q_ssem.at[ch], q_rsem.at[ch], k, o,
                    )
                    copy.start()
                    sends.append(copy)

    def turn(slot):
        act_t[slot] = jnp.transpose(act_full[slot])

    def add_q(ch, slot):
        rows = pl.ds(ch * HALF, HALF)
        q_acc[rows, :] += dot(act_full[slot, rows], w_full[slot], NN)

    scale = HD ** (-0.5)
    heads = g_v.shape[1] // HD

    def slot_of(i):
        dx = i // 2
        dx = jnp.where(dx == 2, 3, jnp.where(dx == 3, 2, dx))
        dc = lax.rem(i, 2)
        return dx * 2 + dc, mod4(x - dx) * 2 + lax.rem(core + dc, 2)

    def dq_copy(ch, k, j):
        rows = pl.ds(ch * PART, PART)
        return owner_copy(
            dq_send.at[j, rows], dq_recv.at[s, rows], dq_ssem.at[ch], dq_rsem.at[ch], k, j
        )

    def stacked(parts):
        return jnp.concatenate(parts, axis=0)

    def col(h):
        return slice(h * HD, (h + 1) * HD)

    def pg_step(j, carry):
        for h in range(heads):
            v = dot(g_recv[j, :, col(h)], kv_v[j, 1, :, col(h)], NT)
            for ch in both:
                pg_v[j, ch, h * PART:(h + 1) * PART, :] = v[ch * PART:(ch + 1) * PART, :]
        return carry

    def attend_one(ch, j):
        rows = slice(ch * PART, (ch + 1) * PART)
        live = ids_ref[pl.ds(j, 1), :] != 0
        sc = stacked(
            [dot(q_recv[j, rows, col(h)], kv_v[j, 0, :, col(h)], NT) for h in range(heads)]
        )
        sc = jnp.where(live, sc * scale, -1e30)
        ex = jnp.exp(sc - jnp.max(sc, axis=1, keepdims=True))
        probs = ex / jnp.sum(ex, axis=1, keepdims=True)
        pg = pg_v[j, ch]
        center = jnp.sum(probs * pg, axis=1, keepdims=True)
        sg = (probs * (pg - center) * scale).astype(BF)
        low = probs.astype(BF)
        for h in range(heads):
            part = slice(h * PART, (h + 1) * PART)
            dq_send[j, rows, col(h)] = dot(sg[part], kv_v[j, 0, :, col(h)], NN).astype(BF)
            probs_v[j, h, rows, :] = low[part]
            sg_v[j, h, rows, :] = sg[part]

    def attend(ch, first, last):
        def chip_step(i, carry):
            k0, j0 = slot_of(2 * i)
            k1, j1 = slot_of(2 * i + 1)

            def wait(k):
                owner_copy(
                    q_send.at[ch, k], q_recv.at[s, pl.ds(ch * PART, PART)],
                    q_ssem.at[ch], q_rsem.at[ch], k, sib["seq"],
                ).wait_recv()

            @pl.when(i > 0)
            def _():
                wait(k0)

            wait(k1)
            attend_one(ch, j0)
            attend_one(ch, j1)

            @pl.when(i > 0)
            def _():
                dq_copy(ch, k0, j0).start()

            dq_copy(ch, k1, j1).start()
            return carry

        lax.fori_loop(first, last, chip_step, 0)

    def dq_in(ch):
        mine = slice(ch * PART, (ch + 1) * PART)
        dq_recv[s, mine, :] = dq_send[s, mine, :]
        for k in range(1, 8):
            dq_copy(ch, k, sib["seq"]).wait_recv()
        for c in range(4):
            v = jnp.zeros((PART, g_v.shape[1]), BF)
            for o in range(8):
                v = jnp.where(names[c] == o, dq_recv[o, ch * PART:(ch + 1) * PART, :], v)
            dq_v[ch * HALF + c * PART:ch * HALF + (c + 1) * PART, :] = v

    def kv_copy(j):
        return pltpu.make_async_copy(kv_v.at[j], kv_out.at[j], kv_sems.at[j])

    def kv_step(j, carry):
        for h in range(heads):
            cols = slice(h * HD, (h + 1) * HD)
            kv_v[j, 0, :, cols] = dot(sg_v[j, h], q_recv[j, :, cols], TN).astype(BF)
            kv_v[j, 1, :, cols] = dot(probs_v[j, h], g_recv[j, :, cols], TN).astype(BF)
        kv_copy(j).start()
        return carry

    def part_act(dest, ch):
        return dot(dq_v[ch * HALF:(ch + 1) * HALF, :], w_full[mod8(dest)], NT)

    def sub_of(value, sub):
        return value[sub * QUART:(sub + 1) * QUART, :]

    zb = {}

    def z_push(ch, d, dist, sub, value):
        n = len(zb)
        z_send[n] = value.astype(BF)
        zb[ch, d, dist, sub] = (push(z_send.at[n], z_recv.at[n], z_dev[d]), n)

    def z_got(ch, d, dist, sub):
        copy, n = zb[ch, d, dist, sub]
        copy.wait_recv()
        return z_recv[n].astype(F32)

    def z_start(ch):
        v = part_act(z + 4, ch)
        z_push(ch, 1, 4, 0, sub_of(v, 0))
        z_push(ch, -1, 4, 1, sub_of(v, 1))
        for e, d in enumerate((1, -1)):
            v = part_act(z + 3 * d, ch)
            z_push(ch, d, 3, 1 - e, sub_of(v, 1 - e))
            pend[ch, e, 0] = sub_of(v, e)

    def z_add(ch, dist, sub):
        for e, d in enumerate((1, -1)):
            sb = sub if d == 1 else 1 - sub
            if sub == 1:
                v = part_act(z + d * (dist - 1), ch)
                pend[ch, e, 1] = sub_of(v, sb)
                pend[ch, e, 0] = sub_of(v, 1 - sb)
            z_push(ch, d, dist - 1, sb, z_got(ch, d, dist, sb) + pend[ch, e, sub])

    def z_end(ch):
        own = part_act(z, ch)
        for sub in (1, 0):
            v = sub_of(own, sub) + z_got(ch, 1, 1, sub) + z_got(ch, -1, 1, sub)
            for c in (0, 1):
                at = (sub * 2 + c) * SPAN + ch * PART
                act_out[at:at + PART, :] = v[c * PART:(c + 1) * PART, :].astype(BF)

    ld_g.wait()
    g_pick()
    ld_w.wait()
    for h in both:
        w_p1_hop1(h)
    z_fwd(0, 0, 0)
    z_fwd(0, 0, 1)
    for h in both:
        w_p2_hop1(h, 0)
    for h in both:
        w_p1_hop2(h)
    q_acc[...] = jnp.zeros_like(q_acc)
    for h in both:
        w_p2_hop1(h, -1)
        w_p2_hop1(h, 1)
    z_fwd(0, 1, 0)
    for h in both:
        w_p2_hop2(h, 0)
    z_fwd(0, 1, 1)
    for h in both:
        w_p2_hop1(h, 2)
    g_copies = g_out()
    for h in both:
        w_p2_hop2(h, -1)
        w_p2_hop2(h, 1)
    z_fwd(0, 2, 0)
    z_fwd(1, 0, 0)
    for h in both:
        w_p2_hop2(h, 2)
    z_fwd(0, 2, 1)
    z_fwd(1, 0, 1)
    for d in sib_w:
        d.wait_recv()
    for k in (0, 1, -1, 2, -2, 3, -3):
        add_q(0, mod8(z + k))
    z_fwd(0, 3, 0)
    z_fwd(0, 3, 1)
    add_q(0, mod8(z + 4))
    q_out(0)
    z_fwd(1, 1, 0)
    z_fwd(1, 1, 1)
    ld_kv.wait()
    for k in range(1, 8):
        g_copies[k].wait_recv()
    lax.fori_loop(0, 8, pg_step, 0)
    z_fwd(1, 2, 0)
    attend(0, 0, 4)
    z_fwd(1, 2, 1)
    for k in (0, 1, -1, 2, -2, 3, -3):
        add_q(1, mod8(z + k))
    dq_in(0)
    z_start(0)
    z_fwd(1, 3, 0)
    z_fwd(1, 3, 1)
    add_q(1, mod8(z + 4))
    q_out(1)
    for k in (0, 1, -1, 2):
        turn(mod8(z + k))
    z_add(0, 4, 0)
    for k in (-2, 3, -3, 4):
        turn(mod8(z + k))
    attend(1, 0, 3)
    z_add(0, 3, 1)
    attend(1, 3, 4)

    def kv_steps(first, last):
        lax.fori_loop(first, last, kv_step, 0)

    kv_steps(0, 3)
    z_add(0, 3, 0)
    dq_in(1)

    order = [(kx, 2) for kx in (2, 1, 3, 0)] + [(2, ky) for ky in (1, 3, 0)]
    order += [(kx, ky) for kx in (1, 3, 0) for ky in (1, 3, 0)]

    def part_w(kx, ky, c):
        rows = pl.ds(pl.multiple_of(mod4(y + ky) * BLK, BLK), BLK)
        return dot(act_t[mod4(x + kx) * 2 + c, rows], dq_v[...], NN)

    sib_d = {}

    def sib_push(n):
        kx, ky = order[n]
        sib_send[n] = part_w(kx, ky, 1 - core).astype(BF)
        sib_d[kx, ky] = (push(sib_send.at[n], red.at[n], sib), n)

    def red_at(h, kf, ku, off, n):
        kx, ky = (kf, ku) if h == 0 else (ku, kf)
        return red.at[order.index((kx % 4, ky % 4)), pl.ds(h * HALF + off, n)]

    def pair_sum(kx, ky):
        copy, n = sib_d[kx, ky]
        copy.wait_recv()
        red[n] = (red[n].astype(F32) + part_w(kx, ky, core)).astype(BF)

    first_ax = {0: y_dev, 1: x_dev}
    second_ax = {0: x_dev, 1: y_dev}
    c1q, c1h, c2q, c2h = {}, {}, {}, {}

    def quarter1(h, kf):
        c1q[h, 1, kf] = push(red_at(h, kf, 2, 0, QUART), p1q.at[h, 0, kf], first_ax[h][1])
        c1q[h, -1, kf] = push(red_at(h, kf, 2, QUART, QUART), p1q.at[h, 1, kf], first_ax[h][-1])

    def half1(h, kf):
        for e, d in enumerate((1, -1)):
            c1q[h, d, kf].wait_recv()
            src = red_at(h, kf, d, 0, HALF)
            got = p1q[h, e, kf].astype(F32)
            lo = src[:QUART].astype(F32)
            hi = src[QUART:].astype(F32)
            lo, hi = (lo + got, hi) if d == 1 else (lo, hi + got)
            s1h[h, e, kf, :QUART] = lo.astype(BF)
            s1h[h, e, kf, QUART:] = hi.astype(BF)
            c1h[h, d, kf] = push(s1h.at[h, e, kf], p1h.at[h, e, kf], first_ax[h][d])

    def final1(h, kf):
        for d in (1, -1):
            c1h[h, d, kf].wait_recv()
        v = red_at(h, kf, 0, 0, HALF)[...].astype(F32)
        v = v + p1h[h, 0, kf].astype(F32) + p1h[h, 1, kf].astype(F32)
        if kf == 2:
            f1b[h] = v.astype(BF)
            c2q[h, 1] = push(f1b.at[h, pl.ds(0, QUART)], p2q.at[h, 0], second_ax[h][1])
            c2q[h, -1] = push(f1b.at[h, pl.ds(QUART, QUART)], p2q.at[h, 1], second_ax[h][-1])
        else:
            f1[h, kf] = v

    def half2(h):
        for e, d in enumerate((1, -1)):
            c2q[h, d].wait_recv()
            got = p2q[h, e].astype(F32)
            lo = f1[h, d % 4, :QUART]
            hi = f1[h, d % 4, QUART:]
            lo, hi = (lo + got, hi) if d == 1 else (lo, hi + got)
            s2h[h, e, :QUART] = lo.astype(BF)
            s2h[h, e, QUART:] = hi.astype(BF)
            c2h[h, d] = push(s2h.at[h, e], p2h.at[h, e], second_ax[h][d])

    def final2(h):
        for d in (1, -1):
            c2h[h, d].wait_recv()
        w_out[h * HALF:(h + 1) * HALF, :] = (
            f1[h, 0] + p2h[h, 0].astype(F32) + p2h[h, 1].astype(F32)
        )

    def sums(first, last):
        for n in range(first, last):
            kx, ky = order[n]
            pair_sum(kx, ky)
            if ky == 2:
                quarter1(0, kx)
            if kx == 2:
                quarter1(1, ky)

    def halves1(kf):
        for h in both:
            half1(h, kf)

    for n in range(7):
        sib_push(n)
    z_add(0, 2, 1)
    sums(0, 4)
    z_add(0, 2, 0)
    z_start(1)
    sums(4, 7)
    for n in range(7, 16):
        sib_push(n)
    halves1(2)
    sums(7, 12)
    z_add(1, 4, 0)
    halves1(1)
    sums(12, 16)
    z_add(1, 3, 1)
    halves1(3)
    halves1(0)
    for h in both:
        final1(h, 2)
    z_end(0)
    z_add(1, 3, 0)
    for h in both:
        final1(h, 1)
    z_add(1, 2, 1)
    for h in both:
        final1(h, 3)
    for h in both:
        half2(h)
    z_add(1, 2, 0)
    for h in both:
        final1(h, 0)
    kv_steps(3, 8)
    for h in both:
        final2(h)
    out_w = pltpu.make_async_copy(w_out, w_o, out_sems.at[0])
    out_w.start()
    z_end(1)
    out_act = pltpu.make_async_copy(act_out, act_o, out_sems.at[1])
    out_act.start()

    for d in sends:
        d.wait_send()
    out_w.wait()
    out_act.wait()
    for k in range(8):
        if k:
            for ch in both:
                dq_copy(ch, k, sib["seq"]).wait_send()
        kv_copy(k).wait()


def tail(act_ref, w_ref, kv_ref, act_out, w_out, kv_out, act_v, w_v, kv_v, in_sems, out_sems):
    moves = [(act_ref, act_v, act_out), (w_ref, w_v, w_out)]
    moves += [(kv_ref.at[j], kv_v.at[j], kv_out.at[j]) for j in range(kv_v.shape[0])]
    come = [
        pltpu.make_async_copy(src, mid, in_sems.at[n]) for n, (src, mid, _) in enumerate(moves)
    ]
    go = [
        pltpu.make_async_copy(mid, dst, out_sems.at[n]) for n, (_, mid, dst) in enumerate(moves)
    ]
    for copy in come:
        copy.start()
    for first, second in zip(come, go):
        first.wait()
        second.start()
    for copy in go:
        copy.wait()


def on_device(span_act, q_weight, out_grad, neighbour_kv, neighbour_ids, owner):
    tok, width = out_grad.shape
    dcol = span_act.shape[1]
    half, quart = tok // 2, tok // 4
    any_spec = pl.BlockSpec(memory_space=pl.ANY)
    vmem = pl.BlockSpec(memory_space=pltpu.VMEM)
    hbm = pl.BlockSpec(memory_space=pltpu.HBM)

    def bf(*shape):
        return pltpu.VMEM(shape, BF)

    def f32(*shape):
        return pltpu.VMEM(shape, F32)

    shapes = (
        jax.ShapeDtypeStruct((tok, dcol), BF),
        jax.ShapeDtypeStruct((q_weight.shape[0], width), F32),
        jax.ShapeDtypeStruct(neighbour_kv.shape, BF),
    )
    results = pl.pallas_call(
        kernel,
        out_shape=shapes,
        in_specs=[any_spec, any_spec, any_spec, any_spec, vmem,
                  pl.BlockSpec(memory_space=pltpu.SMEM)],
        out_specs=(any_spec,) * 3,
        scratch_shapes=[
            bf(tok, dcol), f32(tok, width),
            bf(8, tok, dcol), bf(8, dcol, tok), bf(8, dcol, width),
            bf(*neighbour_kv.shape), f32(8, 2, width // HD * SPAN // 2, KEYS), bf(8, width // HD, SPAN, KEYS), bf(8, width // HD, SPAN, KEYS),
            bf(tok, width), f32(tok, width), bf(tok, width),
            bf(2, 8, SPAN // 2, width), bf(8, SPAN, width), bf(8, SPAN, width), bf(8, SPAN, width),
            bf(8, SPAN, width), bf(8, SPAN, width), bf(tok, width),
            bf(28, quart, dcol), bf(28, quart, dcol), f32(2, 2, 2, quart, dcol),
            bf(16, tok, width), bf(16, tok, width),
            bf(2, 2, 4, quart, width), bf(2, 2, 4, half, width), bf(2, 2, 4, half, width),
            f32(2, 4, half, width), bf(2, half, width), bf(2, 2, half, width),
            bf(2, 2, quart, width), bf(2, 2, half, width),
            pltpu.SemaphoreType.DMA((200,)), pltpu.SemaphoreType.DMA((200,)),
            *[pltpu.SemaphoreType.DMA((8,))] * 2, *[pltpu.SemaphoreType.DMA((2, 8))] * 4,
            pltpu.SemaphoreType.DMA((11,)), pltpu.SemaphoreType.DMA((8,)),
            pltpu.SemaphoreType.DMA((2,)),
        ],
        compiler_params=pltpu.CompilerParams(
            collective_id=0, has_side_effects=True, vmem_limit_bytes=60 * 1024 * 1024
        ),
        cost_estimate=pl.CostEstimate(
            flops=8 * 10**9, bytes_accessed=16 * 2**20, transcendentals=600000
        ),
    )(span_act, q_weight, out_grad, neighbour_kv, neighbour_ids, owner)
    return pl.pallas_call(
        tail,
        out_shape=shapes,
        in_specs=[hbm] * 3,
        out_specs=(hbm,) * 3,
        scratch_shapes=[
            bf(tok, dcol), f32(q_weight.shape[0], width), bf(*neighbour_kv.shape),
            pltpu.SemaphoreType.DMA((10,)), pltpu.SemaphoreType.DMA((10,)),
        ],
        compiler_params=pltpu.CompilerParams(vmem_limit_bytes=60 * 1024 * 1024),
    )(*results)


def solution(mesh):
    in_specs = (
        P(("seq", "dp"), "tensor"),
        P(("seq", "dp"), "tensor"),
        P(("seq", "dp"), "tensor"),
        P(("seq", "dp"), None, None, "tensor"),
        P(("seq", "dp"), None),
        P(),
    )
    out_specs = (
        P(("seq", "dp"), "tensor"),
        P(("seq", "dp"), "tensor"),
        P(("seq", "dp"), None, None, "tensor"),
    )
    return jax.shard_map(
        on_device, mesh=mesh, in_specs=in_specs, out_specs=out_specs, check_vma=False
    )
```

time: 133 us -> 113 us (0.85); the launches traced: 131 us -> 113 us
  Pallas kernels: 122 us -> 112 us
  local copies, waits for them, and re-layouts: 8.31 us -> 0 us
    pallas_call x1 -> x2, Pallas kernels: 122 us -> 112 us  [the longest x1 107 us: on_device(): pl.pallas_call(kernel, out_shape=shapes, in_specs=[any_spec, any_spec, an...]
    unnamed x3 -> x0, local copies, waits for them, and re-layouts: 8.31 us -> none
where the time goes in v3:
time: 113 us
  Pallas kernels  112 us (99%)
    pallas_call x1, Pallas kernels, on_device(): pl.pallas_call(kernel, out_shape=shapes, in_specs=[any_spec, any_spec, an...  107 us
    pallas_call x1, Pallas kernels, on_device(): pl.pallas_call(tail, out_shape=shapes, in_specs=[hbm] * 3, out_specs=(hbm...  4.71 us

profile of v3, /device:TPU:2, one launch (start us, length us, event | category | flops | bytes accessed | tf_op | source)
XLA Modules:
  0.0 112.7 jit_solution(2711495061104695952)
XLA Ops:
  0.6 107.2 %shard_map.85 = (bf16[256,1024]{1,0:T(8,128)(2,1)}, f32[256,512]{1,0:T(8,128)}, bf16[8,2,256,512]{3,2,1,0:T(8,128)(2,1)}) custom-call(bf16[256,1024]{1,0:T(8,128)(2,1)} %act_ref.1, bf16[256,512]{1,0:T(8,128)(2,1)} %w_ref.1, bf16[256,512]{1,0:T(8,128)(2,1)} %g_ref.1, bf16[8,2,256,512]{3,2,1,0:T(8,128)(2,1)} %kv_ref.1, s32[8,256]{1,0:T(8,128)} %ids_ref.1, ...), custom_call_target="tpu_custom_call" | custom-call | flops 8000000000 | bytes 16777216 | tf_op jit(solution)/shard_map/pallas_call | solution.py:643
  107.8 4.7 %shard_map.86 = (bf16[256,1024]{1,0:T(8,128)(2,1)}, f32[256,512]{1,0:T(8,128)}, bf16[8,2,256,512]{3,2,1,0:T(8,128)(2,1)}) custom-call(bf16[256,1024]{1,0:T(8,128)(2,1)} %get-tuple-element.6.act_ref, f32[256,512]{1,0:T(8,128)} %get-tuple-element.7.w_ref, bf16[8,2,256,512]{3,2,1,0:T(8,128)(2,1)} %get-tuple-element.8.kv_ref), custom_call_target="tpu_custom_call" | custom-call | tf_op jit(solution)/shard_map/pallas_call | solution.py:673

commit v4 on v3

--- a/solution.py
+++ b/solution.py
@@ -140,12 +140,12 @@
     wp1, wp1b, wp2, wp2b = {}, {}, {}, {}
 
     def w_start_p1(h):
-        src = w_ref.at[pl.ds(h * HALF, HALF)]
+        src = w_ref_at(h, 0, 0, 0, HALF)
         for d in (1, -1):
             wp1[h, d] = push(src, w_ref_at(h, 0, 0, 0, HALF), ax[h][0][d])
 
     def w_start_p2(h):
-        src = w_ref.at[pl.ds(h * HALF, HALF)]
+        src = w_ref_at(h, 0, 0, 0, HALF)
         for d in (1, -1):
             wp2[h, 0, d] = push(src, w_ref_at(h, 0, 0, 0, HALF), ax[h][1][d])
 
@@ -182,6 +182,7 @@
 
     both = (0, 1)
     z_first(0)
+    ld_w.wait()
     for h in both:
         w_start_p1(h)
     for h in both:
@@ -189,7 +190,7 @@
     for d in ld_act:
         d.wait()
     z_first(1)
-    sib_w.append(push(w_ref, w_full.at[s, own_rows], sib))
+    sib_w.append(push(w_full.at[s, own_rows], w_full.at[s, own_rows], sib))
 
     block = s * 4 + y
     names = [owner_ref[block * 4 + c] for c in range(4)]
@@ -281,24 +282,30 @@
                 pg_v[j, ch, h * PART:(h + 1) * PART, :] = v[ch * PART:(ch + 1) * PART, :]
         return carry
 
-    def attend_one(ch, j):
+    def attend_slots(ch, slots):
         rows = slice(ch * PART, (ch + 1) * PART)
-        live = ids_ref[pl.ds(j, 1), :] != 0
-        sc = stacked(
-            [dot(q_recv[j, rows, col(h)], kv_v[j, 0, :, col(h)], NT) for h in range(heads)]
-        )
-        sc = jnp.where(live, sc * scale, -1e30)
-        ex = jnp.exp(sc - jnp.max(sc, axis=1, keepdims=True))
-        probs = ex / jnp.sum(ex, axis=1, keepdims=True)
-        pg = pg_v[j, ch]
-        center = jnp.sum(probs * pg, axis=1, keepdims=True)
-        sg = (probs * (pg - center) * scale).astype(BF)
-        low = probs.astype(BF)
-        for h in range(heads):
-            part = slice(h * PART, (h + 1) * PART)
-            dq_send[j, rows, col(h)] = dot(sg[part], kv_v[j, 0, :, col(h)], NN).astype(BF)
-            probs_v[j, h, rows, :] = low[part]
-            sg_v[j, h, rows, :] = sg[part]
+        parts = [slice(h * PART, (h + 1) * PART) for h in range(heads)]
+        scores = [
+            stacked([dot(q_recv[j, rows, col(h)], kv_v[j, 0, :, col(h)], NT) for h in range(heads)])
+            for j in slots
+        ]
+        grads = []
+        for j, sc in zip(slots, scores):
+            live = ids_ref[pl.ds(j, 1), :] != 0
+            sc = jnp.where(live, sc * scale, -1e30)
+            ex = jnp.exp(sc - jnp.max(sc, axis=1, keepdims=True))
+            pg = pg_v[j, ch]
+            recip = 1.0 / jnp.sum(ex, axis=1, keepdims=True)
+            center = jnp.sum(ex * pg, axis=1, keepdims=True) * recip
+            probs = ex * recip
+            grads.append((probs.astype(BF), (probs * (pg - center) * scale).astype(BF)))
+        for j, (_, sg) in zip(slots, grads):
+            for h in range(heads):
+                dq_send[j, rows, col(h)] = dot(sg[parts[h]], kv_v[j, 0, :, col(h)], NN).astype(BF)
+        for j, (low, sg) in zip(slots, grads):
+            for h in range(heads):
+                probs_v[j, h, rows, :] = low[parts[h]]
+                sg_v[j, h, rows, :] = sg[parts[h]]
 
     def attend(ch, first, last):
         def chip_step(i, carry):
@@ -316,8 +323,7 @@
                 wait(k0)
 
             wait(k1)
-            attend_one(ch, j0)
-            attend_one(ch, j1)
+            attend_slots(ch, (j0, j1))
 
             @pl.when(i > 0)
             def _():
@@ -396,7 +402,6 @@
 
     ld_g.wait()
     g_pick()
-    ld_w.wait()
     for h in both:
         w_p1_hop1(h)
     z_fwd(0, 0, 0)

time: 113 us -> 109 us (0.965)
  Pallas kernels: 112 us -> 108 us
    pallas_call x1, Pallas kernels: 107 us -> 104 us  [on_device(): pl.pallas_call(kernel, out_shape=shapes, in_specs=[any_spec, any_spec, an...]
where the time goes in v4:
time: 109 us
  Pallas kernels  108 us (99%)
    pallas_call x1, Pallas kernels, on_device(): pl.pallas_call(kernel, out_shape=shapes, in_specs=[any_spec, any_spec, an...  104 us
    pallas_call x1, Pallas kernels, on_device(): pl.pallas_call(tail, out_shape=shapes, in_specs=[hbm] * 3, out_specs=(hbm...  4.71 us

profile of v4, /device:TPU:2, one launch (start us, length us, event | category | flops | bytes accessed | tf_op | source)
XLA Modules:
  0.0 109.0 jit_solution(9833361577898518568)
XLA Ops:
  0.6 103.7 %shard_map.85 = (bf16[256,1024]{1,0:T(8,128)(2,1)}, f32[256,512]{1,0:T(8,128)}, bf16[8,2,256,512]{3,2,1,0:T(8,128)(2,1)}) custom-call(bf16[256,1024]{1,0:T(8,128)(2,1)} %act_ref.1, bf16[256,512]{1,0:T(8,128)(2,1)} %w_ref.1, bf16[256,512]{1,0:T(8,128)(2,1)} %g_ref.1, bf16[8,2,256,512]{3,2,1,0:T(8,128)(2,1)} %kv_ref.1, s32[8,256]{1,0:T(8,128)} %ids_ref.1, ...), custom_call_target="tpu_custom_call" | custom-call | flops 8000000000 | bytes 16777216 | tf_op jit(solution)/shard_map/pallas_call | solution.py:648
  104.3 4.7 %shard_map.86 = (bf16[256,1024]{1,0:T(8,128)(2,1)}, f32[256,512]{1,0:T(8,128)}, bf16[8,2,256,512]{3,2,1,0:T(8,128)(2,1)}) custom-call(bf16[256,1024]{1,0:T(8,128)(2,1)} %get-tuple-element.6.act_ref, f32[256,512]{1,0:T(8,128)} %get-tuple-element.7.w_ref, bf16[8,2,256,512]{3,2,1,0:T(8,128)(2,1)} %get-tuple-element.8.kv_ref), custom_call_target="tpu_custom_call" | custom-call | tf_op jit(solution)/shard_map/pallas_call | solution.py:678

commit v5 on v4

--- a/solution.py
+++ b/solution.py
@@ -439,13 +439,14 @@
     add_q(0, mod8(z + 4))
     q_out(0)
     z_fwd(1, 1, 0)
-    z_fwd(1, 1, 1)
     ld_kv.wait()
     for k in range(1, 8):
         g_copies[k].wait_recv()
     lax.fori_loop(0, 8, pg_step, 0)
+    z_fwd(1, 1, 1)
+    attend(0, 0, 2)
     z_fwd(1, 2, 0)
-    attend(0, 0, 4)
+    attend(0, 2, 4)
     z_fwd(1, 2, 1)
     for k in (0, 1, -1, 2, -2, 3, -3):
         add_q(1, mod8(z + k))

time: 109 us -> 108 us (level)
    pallas_call x1, Pallas kernels: 104 us -> 102 us  [on_device(): pl.pallas_call(kernel, out_shape=shapes, in_specs=[any_spec, any_spec, an...]
where the time goes in v5:
time: 108 us; the launch traced here: 107 us
  Pallas kernels  107 us (99%)
    pallas_call x1, Pallas kernels, on_device(): pl.pallas_call(kernel, out_shape=shapes, in_specs=[any_spec, any_spec, an...  102 us
    pallas_call x1, Pallas kernels, on_device(): pl.pallas_call(tail, out_shape=shapes, in_specs=[hbm] * 3, out_specs=(hbm...  4.71 us

profile of v5, /device:TPU:2, one launch (start us, length us, event | category | flops | bytes accessed | tf_op | source)
XLA Modules:
  0.0 107.5 jit_solution(12848919162002937641)
XLA Ops:
  0.6 102.0 %shard_map.85 = (bf16[256,1024]{1,0:T(8,128)(2,1)}, f32[256,512]{1,0:T(8,128)}, bf16[8,2,256,512]{3,2,1,0:T(8,128)(2,1)}) custom-call(bf16[256,1024]{1,0:T(8,128)(2,1)} %act_ref.1, bf16[256,512]{1,0:T(8,128)(2,1)} %w_ref.1, bf16[256,512]{1,0:T(8,128)(2,1)} %g_ref.1, bf16[8,2,256,512]{3,2,1,0:T(8,128)(2,1)} %kv_ref.1, s32[8,256]{1,0:T(8,128)} %ids_ref.1, ...), custom_call_target="tpu_custom_call" | custom-call | flops 8000000000 | bytes 16777216 | tf_op jit(solution)/shard_map/pallas_call | solution.py:649
  102.6 4.7 %shard_map.86 = (bf16[256,1024]{1,0:T(8,128)(2,1)}, f32[256,512]{1,0:T(8,128)}, bf16[8,2,256,512]{3,2,1,0:T(8,128)(2,1)}) custom-call(bf16[256,1024]{1,0:T(8,128)(2,1)} %get-tuple-element.6.act_ref, f32[256,512]{1,0:T(8,128)} %get-tuple-element.7.w_ref, bf16[8,2,256,512]{3,2,1,0:T(8,128)(2,1)} %get-tuple-element.8.kv_ref), custom_call_target="tpu_custom_call" | custom-call | tf_op jit(solution)/shard_map/pallas_call | solution.py:679

commit v6 on v5

--- a/solution.py
+++ b/solution.py
@@ -558,9 +558,11 @@
         for h in both:
             half1(h, kf)
 
-    for n in range(7):
+    for n in range(4):
         sib_push(n)
     z_add(0, 2, 1)
+    for n in range(4, 7):
+        sib_push(n)
     sums(0, 4)
     z_add(0, 2, 0)
     z_start(1)

time: 108 us -> 107 us (level)
  no operation moved by 1% of the time
where the time goes in v6:
time: 107 us
  Pallas kernels  106 us (99%)
    pallas_call x1, Pallas kernels, on_device(): pl.pallas_call(kernel, out_shape=shapes, in_specs=[any_spec, any_spec, an...  101 us
    pallas_call x1, Pallas kernels, on_device(): pl.pallas_call(tail, out_shape=shapes, in_specs=[hbm] * 3, out_specs=(hbm...  4.71 us

profile of v6, /device:TPU:2, one launch (start us, length us, event | category | flops | bytes accessed | tf_op | source)
XLA Modules:
  0.0 106.8 jit_solution(15867552945567191606)
XLA Ops:
  0.6 101.3 %shard_map.85 = (bf16[256,1024]{1,0:T(8,128)(2,1)}, f32[256,512]{1,0:T(8,128)}, bf16[8,2,256,512]{3,2,1,0:T(8,128)(2,1)}) custom-call(bf16[256,1024]{1,0:T(8,128)(2,1)} %act_ref.1, bf16[256,512]{1,0:T(8,128)(2,1)} %w_ref.1, bf16[256,512]{1,0:T(8,128)(2,1)} %g_ref.1, bf16[8,2,256,512]{3,2,1,0:T(8,128)(2,1)} %kv_ref.1, s32[8,256]{1,0:T(8,128)} %ids_ref.1, ...), custom_call_target="tpu_custom_call" | custom-call | flops 8000000000 | bytes 16777216 | tf_op jit(solution)/shard_map/pallas_call | solution.py:651
  101.9 4.7 %shard_map.86 = (bf16[256,1024]{1,0:T(8,128)(2,1)}, f32[256,512]{1,0:T(8,128)}, bf16[8,2,256,512]{3,2,1,0:T(8,128)(2,1)}) custom-call(bf16[256,1024]{1,0:T(8,128)(2,1)} %get-tuple-element.6.act_ref, f32[256,512]{1,0:T(8,128)} %get-tuple-element.7.w_ref, bf16[8,2,256,512]{3,2,1,0:T(8,128)(2,1)} %get-tuple-element.8.kv_ref), custom_call_target="tpu_custom_call" | custom-call | tf_op jit(solution)/shard_map/pallas_call | solution.py:681
